TPU v7x, 32 devices: a whole 2x2x4 slice. The times are simulated.
32 devices in a mesh: dp: 4 (over z), fsdp: 8 (over y, x, core).
Axes of the slice: x: 2, y: 2, z: 4, core: 2. Of those that a mesh axis runs over, the one named last changes fastest.
Arguments:
- frames: bfloat16 [2, 32, 384, 512], P(None, ('dp', 'fsdp')), may hold values from -6 to 6
- upstream: bfloat16 [2, 32, 384, 512], P(None, ('dp', 'fsdp')), may hold values from -6 to 6
- utterance: int32 [2, 32, 24], P(None, ('dp', 'fsdp')), may hold values from 0 to 5, never falling along the last dimension, each value on 1 to 8 neighbouring positions
- first_gain: bfloat16 [512], P('fsdp'), may hold values from 0.099609375 to 1.8984375
- first_shift: bfloat16 [512], P('fsdp'), may hold values from -3 to 3
- project_in: bfloat16 [512, 1536], P('fsdp'), may hold values from -0.25 to 0.25
- query_bias: bfloat16 [512], P('fsdp'), may hold values from -3 to 3
- value_bias: bfloat16 [512], P('fsdp'), may hold values from -3 to 3
- project_out: bfloat16 [512, 512], P('fsdp'), may hold values from -0.75 to 0.75
- out_bias: bfloat16 [512], P('fsdp'), may hold values from -3 to 3
- second_gain: bfloat16 [512], P('fsdp'), may hold values from 0.099609375 to 1.8984375
- second_shift: bfloat16 [512], P('fsdp'), may hold values from -3 to 3
- up_weight: bfloat16 [512, 2048], P('fsdp'), may hold values from -0.25 to 0.25
- up_bias: bfloat16 [2048], P('fsdp'), may hold values from -3 to 3
- down_weight: bfloat16 [2048, 512], P('fsdp'), may hold values from -0.1875 to 0.1875
- down_bias: bfloat16 [512], P('fsdp'), may hold values from -3 to 3
Outputs:
- output: bfloat16 [2, 32, 384, 512], P(None, ('dp', 'fsdp'))
- grad_frames: float32 [2, 32, 384, 512], P(None, ('dp', 'fsdp'))
- grad_first_gain: float32 [512], P('fsdp')
- grad_first_shift: float32 [512], P('fsdp')
- grad_project_in: float32 [512, 1536], P('fsdp')
- grad_query_bias: float32 [512], P('fsdp')
- grad_value_bias: float32 [512], P('fsdp')
- grad_project_out: float32 [512, 512], P('fsdp')
- grad_out_bias: float32 [512], P('fsdp')
- grad_second_gain: float32 [512], P('fsdp')
- grad_second_shift: float32 [512], P('fsdp')
- grad_up_weight: float32 [512, 2048], P('fsdp')
- grad_up_bias: float32 [2048], P('fsdp')
- grad_down_weight: float32 [2048, 512], P('fsdp')
- grad_down_bias: float32 [512], P('fsdp')
Inputs may be any that keep to these rules, and one draw needn't show every extreme that they name: In each packed row the utterance numbers never fall, every utterance covers 1 to 8 consecutive segments, and some utterance covers exactly 8.
All inputs are finite; a program needn't handle non-finite values.
Results may differ from a plain program's by a relative error of at most 0.023.
Values may be sent and summed in bfloat16 or wider, within the bound.
No kernel may reach another device: no remote copies, remote signals or barrier semaphores. Data moves between devices by JAX's collectives and lax.ppermute only.
A program may use at most 192 MiB of HBM per device.

v0:
```python
import jax
import jax.numpy as jnp
from jax import lax
from jax.sharding import PartitionSpec as P

HEADS = 8
SEG = 16
RIGHT = 4
LEFT = 30
MEMS = 4


def round_value(value):
    return lax.optimization_barrier(value.astype(jnp.bfloat16)).astype(jnp.float32)


def make_rounders():

    def value_keep(value):
        return (round_value(value), None)

    def value_pass(kept, grad):
        return (grad,)

    def grad_keep(value):
        return (value, None)

    def grad_round(kept, grad):
        return (round_value(grad),)

    def plain_value(value):
        return value

    round_down = jax.custom_vjp(round_value)
    round_down.defvjp(value_keep, value_pass)
    round_grad = jax.custom_vjp(plain_value)
    round_grad.defvjp(grad_keep, grad_round)
    return (round_down, round_grad)


def layer_norm(value, gain, shift):
    center = jnp.mean(value, axis=-1, keepdims=True)
    offset = value - center
    spread = jnp.mean(offset * offset, axis=-1, keepdims=True)
    return offset * lax.rsqrt(spread + 1e-05) * gain + shift


def matmul(left, right):
    return jnp.dot(left, right, preferred_element_type=jnp.float32)


def row_attention(query, keys, values, mem_keys, mem_values, utter):
    round_down, round_grad = make_rounders()
    length, width = query.shape
    head_width = width // HEADS
    nsegs = utter.shape[0]
    block = min(512, length)
    frame_utt = jnp.repeat(utter, SEG)
    padded_keys = jnp.pad(keys, ((64, 64), (0, 0)))
    padded_vals = jnp.pad(values, ((64, 64), (0, 0)))
    padded_utt = jnp.pad(frame_utt, (64, 64), constant_values=-1)
    memory_key_rows = mem_keys.reshape(nsegs, HEADS, head_width)
    memory_value_rows = mem_values.reshape(nsegs, HEADS, head_width)
    seg_index = jnp.arange(nsegs, dtype=jnp.int32)
    score_scale = 1.0 / head_width**0.5

    def one_block(index):
        start = (index * block).astype(jnp.int32)
        query_tile = lax.dynamic_slice_in_dim(query, start, block, 0).reshape(
            block, HEADS, head_width
        )
        k_block = lax.dynamic_slice_in_dim(padded_keys, start, block + 128, 0).reshape(
            block + 128, HEADS, head_width
        )
        v_block = lax.dynamic_slice_in_dim(padded_vals, start, block + 128, 0).reshape(
            block + 128, HEADS, head_width
        )
        k_utter = lax.dynamic_slice_in_dim(padded_utt, start, block + 128, 0)
        q_utter = lax.dynamic_slice_in_dim(frame_utt, start, block, 0)
        q_place = start + jnp.arange(block, dtype=jnp.int32)
        k_place = start - 64 + jnp.arange(block + 128, dtype=jnp.int32)
        q_seg = q_place // SEG
        lower = q_seg * SEG - LEFT
        upper = q_seg * SEG + SEG + RIGHT
        allowed = (
            (k_utter[None, :] == q_utter[:, None])
            & (k_place[None, :] >= lower[:, None])
            & (k_place[None, :] < upper[:, None])
        )
        mem_ok = (
            (utter[None, :] == q_utter[:, None])
            & (seg_index[None, :] >= q_seg[:, None] - MEMS)
            & (seg_index[None, :] < q_seg[:, None])
        )
        s_frames = (
            jnp.einsum("qhd,khd->hqk", query_tile, k_block, preferred_element_type=jnp.float32)
            * score_scale
        )
        summary_memory = (
            jnp.einsum(
                "wbt,ubt->bwu", query_tile, memory_key_rows, preferred_element_type=jnp.float32
            )
            * score_scale
        )
        s_frames = jnp.where(allowed[None], s_frames, -1000000000.0)
        summary_memory = jnp.where(mem_ok[None], summary_memory, -1000000000.0)
        top = jnp.maximum(
            jnp.max(s_frames, axis=-1, keepdims=True),
            jnp.max(summary_memory, axis=-1, keepdims=True),
        )
        e_frames = jnp.exp(s_frames - top)
        e_memory = jnp.exp(summary_memory - top)
        total = jnp.sum(e_frames, axis=-1, keepdims=True) + jnp.sum(
            e_memory, axis=-1, keepdims=True
        )
        p_frames = round_down(e_frames / total)
        previous_memory = round_down(e_memory / total)
        layer_result = jnp.einsum(
            "hqk,khd->qhd", p_frames, v_block, preferred_element_type=jnp.float32
        )
        layer_result = layer_result + jnp.einsum(
            "elv,vew->lew", previous_memory, memory_value_rows, preferred_element_type=jnp.float32
        )
        return layer_result.reshape(block, width)

    blocks = lax.map(jax.checkpoint(one_block), jnp.arange(length // block, dtype=jnp.int32))
    return blocks.reshape(length, width)


def forward(inputs, utter, params):
    round_down, round_grad = make_rounders()
    (
        first_gain,
        first_shift,
        project_in,
        query_bias,
        value_bias,
        project_out,
        out_bias,
        second_gain,
        second_shift,
        up_weight,
        up_bias,
        down_weight,
        down_bias,
    ) = params
    width = inputs.shape[-1]
    nrows = inputs.shape[0]
    nsegs = inputs.shape[1] // SEG
    normed = round_down(layer_norm(inputs, first_gain, first_shift))
    mixed = matmul(normed, project_in)
    query = round_down(round_grad(mixed[..., :width] + query_bias))
    keys = round_down(round_grad(mixed[..., width : 2 * width]))
    values = round_down(round_grad(mixed[..., 2 * width :] + value_bias))
    summary = round_down(jnp.mean(normed.reshape(nrows, nsegs, SEG, width), axis=2))
    mem_mixed = matmul(summary, project_in[:, width:])
    mem_keys = round_down(round_grad(mem_mixed[..., :width]))
    mem_values = round_down(round_grad(mem_mixed[..., width:] + value_bias))
    attended = jax.vmap(row_attention)(query, keys, values, mem_keys, mem_values, utter)
    attended = round_down(round_grad(attended))
    resid = inputs + matmul(attended, project_out) + out_bias
    normed2 = round_down(layer_norm(resid, second_gain, second_shift))
    hidden = round_down(round_grad(jax.nn.gelu(matmul(normed2, up_weight) + up_bias)))
    return resid + matmul(hidden, down_weight) + down_bias


def widen(pieces):
    return tuple((piece.astype(jnp.float32) for piece in pieces))


def accumulate(total, terms):
    if total is None:
        return terms
    return tuple((left + right for left, right in zip(total, terms)))


def shards(
    frames,
    upstream,
    utterance,
    first_gain,
    first_shift,
    project_in,
    query_bias,
    value_bias,
    project_out,
    out_bias,
    second_gain,
    second_shift,
    up_weight,
    up_bias,
    down_weight,
    down_bias,
):
    micro_count = frames.shape[0]
    outputs = []
    grad_inputs = []
    shares = None
    for micro in range(micro_count):
        inputs = frames[micro].astype(jnp.float32)
        cotangent = upstream[micro].astype(jnp.float32)
        utter = utterance[micro]

        def layer(value, weights, utter=utter):
            return forward(value, utter, weights)

        ahead = (
            lax.all_gather(first_gain, "fsdp", axis=0, tiled=True),
            lax.all_gather(first_shift, "fsdp", axis=0, tiled=True),
            lax.all_gather(project_in, "fsdp", axis=0, tiled=True),
            lax.all_gather(query_bias, "fsdp", axis=0, tiled=True),
            lax.all_gather(value_bias, "fsdp", axis=0, tiled=True),
            lax.all_gather(project_out, "fsdp", axis=0, tiled=True),
            lax.all_gather(out_bias, "fsdp", axis=0, tiled=True),
            lax.all_gather(second_gain, "fsdp", axis=0, tiled=True),
            lax.all_gather(second_shift, "fsdp", axis=0, tiled=True),
            lax.all_gather(up_weight, "fsdp", axis=0, tiled=True),
            lax.all_gather(up_bias, "fsdp", axis=0, tiled=True),
            lax.all_gather(down_weight, "fsdp", axis=0, tiled=True),
            lax.all_gather(down_bias, "fsdp", axis=0, tiled=True),
        )
        layer_result = layer(inputs, widen(ahead))
        again = (
            lax.all_gather(first_gain, "fsdp", axis=0, tiled=True),
            lax.all_gather(first_shift, "fsdp", axis=0, tiled=True),
            lax.all_gather(project_in, "fsdp", axis=0, tiled=True),
            lax.all_gather(query_bias, "fsdp", axis=0, tiled=True),
            lax.all_gather(value_bias, "fsdp", axis=0, tiled=True),
            lax.all_gather(project_out, "fsdp", axis=0, tiled=True),
            lax.all_gather(out_bias, "fsdp", axis=0, tiled=True),
            lax.all_gather(second_gain, "fsdp", axis=0, tiled=True),
            lax.all_gather(second_shift, "fsdp", axis=0, tiled=True),
            lax.all_gather(up_weight, "fsdp", axis=0, tiled=True),
            lax.all_gather(up_bias, "fsdp", axis=0, tiled=True),
            lax.all_gather(down_weight, "fsdp", axis=0, tiled=True),
            lax.all_gather(down_bias, "fsdp", axis=0, tiled=True),
        )
        unused, pull = jax.vjp(layer, inputs, widen(again))
        grad_in, grad_w = pull(cotangent)
        outputs.append(layer_result.astype(jnp.bfloat16))
        grad_inputs.append(grad_in)
        parts = (
            lax.psum_scatter(
                grad_w[0].astype(jnp.bfloat16), "fsdp", scatter_dimension=0, tiled=True
            ).astype(jnp.float32),
            lax.psum_scatter(
                grad_w[1].astype(jnp.bfloat16), "fsdp", scatter_dimension=0, tiled=True
            ).astype(jnp.float32),
            lax.psum_scatter(
                grad_w[2].astype(jnp.bfloat16), "fsdp", scatter_dimension=0, tiled=True
            ).astype(jnp.float32),
            lax.psum_scatter(
                grad_w[3].astype(jnp.bfloat16), "fsdp", scatter_dimension=0, tiled=True
            ).astype(jnp.float32),
            lax.psum_scatter(
                grad_w[4].astype(jnp.bfloat16), "fsdp", scatter_dimension=0, tiled=True
            ).astype(jnp.float32),
            lax.psum_scatter(
                grad_w[5].astype(jnp.bfloat16), "fsdp", scatter_dimension=0, tiled=True
            ).astype(jnp.float32),
            lax.psum_scatter(
                grad_w[6].astype(jnp.bfloat16), "fsdp", scatter_dimension=0, tiled=True
            ).astype(jnp.float32),
            lax.psum_scatter(
                grad_w[7].astype(jnp.bfloat16), "fsdp", scatter_dimension=0, tiled=True
            ).astype(jnp.float32),
            lax.psum_scatter(
                grad_w[8].astype(jnp.bfloat16), "fsdp", scatter_dimension=0, tiled=True
            ).astype(jnp.float32),
            lax.psum_scatter(
                grad_w[9].astype(jnp.bfloat16), "fsdp", scatter_dimension=0, tiled=True
            ).astype(jnp.float32),
            lax.psum_scatter(
                grad_w[10].astype(jnp.bfloat16), "fsdp", scatter_dimension=0, tiled=True
            ).astype(jnp.float32),
            lax.psum_scatter(
                grad_w[11].astype(jnp.bfloat16), "fsdp", scatter_dimension=0, tiled=True
            ).astype(jnp.float32),
            lax.psum_scatter(
                grad_w[12].astype(jnp.bfloat16), "fsdp", scatter_dimension=0, tiled=True
            ).astype(jnp.float32),
        )
        shares = accumulate(shares, tuple(parts))
    totals = (
        lax.psum(shares[0].astype(jnp.bfloat16), "dp").astype(jnp.float32),
        lax.psum(shares[1].astype(jnp.bfloat16), "dp").astype(jnp.float32),
        lax.psum(shares[2].astype(jnp.bfloat16), "dp").astype(jnp.float32),
        lax.psum(shares[3].astype(jnp.bfloat16), "dp").astype(jnp.float32),
        lax.psum(shares[4].astype(jnp.bfloat16), "dp").astype(jnp.float32),
        lax.psum(shares[5].astype(jnp.bfloat16), "dp").astype(jnp.float32),
        lax.psum(shares[6].astype(jnp.bfloat16), "dp").astype(jnp.float32),
        lax.psum(shares[7].astype(jnp.bfloat16), "dp").astype(jnp.float32),
        lax.psum(shares[8].astype(jnp.bfloat16), "dp").astype(jnp.float32),
        lax.psum(shares[9].astype(jnp.bfloat16), "dp").astype(jnp.float32),
        lax.psum(shares[10].astype(jnp.bfloat16), "dp").astype(jnp.float32),
        lax.psum(shares[11].astype(jnp.bfloat16), "dp").astype(jnp.float32),
        lax.psum(shares[12].astype(jnp.bfloat16), "dp").astype(jnp.float32),
    )
    return (
        jnp.stack(outputs),
        jnp.stack(grad_inputs),
        totals[0],
        totals[1],
        totals[2],
        totals[3],
        totals[4],
        totals[5],
        totals[6],
        totals[7],
        totals[8],
        totals[9],
        totals[10],
        totals[11],
        totals[12],
    )


def solution(mesh):
    placed = (
        P(None, ("dp", "fsdp"), None, None),
        P(None, ("dp", "fsdp"), None, None),
        P(None, ("dp", "fsdp"), None),
        P("fsdp"),
        P("fsdp"),
        P("fsdp", None),
        P("fsdp"),
        P("fsdp"),
        P("fsdp", None),
        P("fsdp"),
        P("fsdp"),
        P("fsdp"),
        P("fsdp", None),
        P("fsdp"),
        P("fsdp", None),
        P("fsdp"),
    )
    return jax.shard_map(
        shards,
        mesh=mesh,
        in_specs=placed,
        out_specs=(
            P(None, ("dp", "fsdp"), None, None),
            P(None, ("dp", "fsdp"), None, None),
            P("fsdp"),
            P("fsdp"),
            P("fsdp", None),
            P("fsdp"),
            P("fsdp"),
            P("fsdp", None),
            P("fsdp"),
            P("fsdp"),
            P("fsdp"),
            P("fsdp", None),
            P("fsdp"),
            P("fsdp", None),
            P("fsdp"),
        ),
        check_vma=False,
    )
```

profile of v0, /device:TPU:0, one launch (start us, length us, event | category | flops | bytes accessed | tf_op | source)
XLA Modules:
  0.0 605.4 jit_solution(12879914363415557112)
XLA Ops:
  19.8 15.7 %all-reduce.51 = (bf16[512]{0:T(512)(128)(2,1)S(1)}, bf16[512]{0:T(512)(128)(2,1)S(1)}, bf16[512]{0:T(512)(128)(2,1)S(1)}, bf16[512]{0:T(512)(128)(2,1)S(1)}, bf...) all-reduce(bf16[512]{0:T(512)(128)(2,1)S(1)} %dynamic-update-slice., ...), channel_id=1, replica_groups=mesh['dp'=4,'fsdp'=8] {'fsdp'}, use_global_device_ids=true, to_apply=%add.25 | all-reduce | flops 3584 | bytes 14336
  41.2 7.7 %all-gather = bf16[8,1,256]{2,1,0:T(2,128)(2,1)S(1)} all-gather(bf16[1,1,256]{2,1,0:T(2,128)(2,1)S(1)} %reshape.4359), channel_id=1, replica_groups=mesh['dp'=4,'fsdp'=8] {'fsdp'}, dimensions={0}, use_global_device_ids=true | all-gather | bytes 4608 | tf_op jit(solution)/shard_map/all_gather | solution.py:218
  49.7 10.3 %all_gather.31 = bf16[512,512]{1,0:T(8,128)(2,1)S(1)} all-gather(bf16[64,512]{1,0:T(8,128)(2,1)} %param.36), channel_id=1, replica_groups=mesh['dp'=4,'fsdp'=8] {'fsdp'}, dimensions={0}, use_global_device_ids=true | all-gather | bytes 589824 | tf_op jit(solution)/shard_map/all_gather | solution.py:213
  107.0 3.9 fusion.77
  113.1 7.5 %fusion.379 = (bf16[2048]{0:T(1024)(128)(2,1)}, bf16[1,384,2048]{2,1,0:T(8,128)(2,1)S(1)}, f32[384,2048]{1,0:T(8,128)}) fusion(bf16[1,384,2048]{2,1,0:T(8,128)(2,1)} %fusion.77, f32[2048]{0:T(1024)} %bitcast.597, bf16[512,2048]{1,0:T(8,128)(2,1)} %all-gather.7.cloned.1.call-done, bf16[1,384,512]{2,1,0:T(8,128)(2,1)} %get-tuple-element.784), kind=kOutput, calls=%fused_computation.563 | convolution fusion | flops 823392256 | bytes 8794112 | tf_op jit(solution)/shard_map/dot_general | solution.py:49
  123.4 5.5 fusion.377
  178.4 7.1 %convert_reduce_fusion.1 = (f32[8,384]{1,0:T(8,128)}, pred[8,384,512]{2,1,0:T(32,128)(4,1)}, f32[8,384]{1,0:T(8,128)S(1)}, f32[8,384,512]{2,1,0:T(8,128)}) fusion(f32[8,384]{1,0:T(8,128)S(1)} %get-tuple-element.821, f32[8,384,512]{2,1,0:T(8,128)S(1)} %get-tuple-element.822, pred[384,512]{1,0:T(8,128)(4,1)S(1)} %compare_and_fusion.5, f32[8,384]{1,0:T(8,128)S(1)} %max.67, ...), kind=kOutput, calls=%fused_computation.8 | convolution fusion | flops 215476224 | bytes 15331328 | tf_op jit(solution)/shard_map/transpose(jvp(vmap()))/while/body/eval_jaxpr/checkpoint/hqk,khd->qhd/dot_general | solution.py:118
  186.9 7.1 %convert_reduce_fusion = (f32[8,384]{1,0:T(8,128)}, pred[8,384,512]{2,1,0:T(32,128)(4,1)}, f32[8,384]{1,0:T(8,128)S(1)}, f32[8,384,512]{2,1,0:T(8,128)}) fusion(f32[8,384]{1,0:T(8,128)S(1)} %get-tuple-element.815, f32[8,384,512]{2,1,0:T(8,128)S(1)} %get-tuple-element.816, pred[384,512]{1,0:T(8,128)(4,1)S(1)} %compare_and_fusion.4, f32[8,384]{1,0:T(8,128)S(1)} %max.69, ...), kind=kOutput, calls=%fused_computation.1 | convolution fusion | flops 215476224 | bytes 15331328 | tf_op jit(solution)/shard_map/transpose(jvp(vmap()))/while/body/eval_jaxpr/checkpoint/hqk,khd->qhd/dot_general | solution.py:118
  198.2 17.4 %fusion.383 = (f32[8,384]{1,0:T(8,128)}, f32[8,384,512]{2,1,0:T(8,128)}, bf16[1,8,384,512]{3,2,1,0:T(8,128)(2,1)S(1)}, bf16[1,8,384,512]{3,2,1,0:T(8,128)(2,1)},...) fusion(f32[8,384]{1,0:T(8,128)} %copy-done.69, f32[8,384,512]{2,1,0:T(8,128)} %copy-done.1, ...), kind=kLoop, calls=%fused_computation.565 | loop fusion | flops 28305408 | bytes 44531712 | tf_op jit(solution)/shard_map/transpose(jvp(vmap()))/while/body/eval_jaxpr/checkpoint/reduce_sum | solution.py:111
  232.2 6.3 %fusion.10 = f32[8,384,64]{1,2,0:T(8,128)} fusion(bf16[512,8,64]{0,2,1:T(8,128)(2,1)} %bitcast.568, f32[8,384,512]{2,1,0:T(8,128)} %get-tuple-element.833, pred[8,384,512]{2,1,0:T(32,128)(4,1)} %get-tuple-element.749, f32[8,384]{1,0:T(8,128)} %get-tuple-element.777, pred[384,512]{1,0:T(8,128)(4,1)} %copy-done.28), kind=kOutput, calls=%fused_computation.34 | convolution fusion | flops 207618048 | bytes 9383936 | tf_op jit(solution)/shard_map/transpose(jvp(vmap()))/while/body/eval_jaxpr/checkpoint/qhd,khd->hqk/dot_general | solution.py:96
  239.9 6.7 %fusion.157 = bf16[8,512,64]{1,2,0:T(8,128)(2,1)} fusion(bf16[384,8,64]{0,2,1:T(8,128)(2,1)} %bitcast.559, f32[8,384,512]{2,1,0:T(8,128)} %get-tuple-element.833, pred[8,384,512]{2,1,0:T(32,128)(4,1)} %get-tuple-element.749, f32[8,384]{1,0:T(8,128)} %get-tuple-element.777, pred[384,512]{1,0:T(8,128)(4,1)} %copy-done.28, pred[]{:T(512)} %get-tuple-element.835), kind=kOutput, calls=%fused_computation.172 | convolution fusion | flops 207880192 | bytes 8990721 | tf_op jit(solution)/shard_map/transpose(jvp(vmap()))/while/body/eval_jaxpr/checkpoint/qhd,khd->hqk/dot_general | solution.py:96
  257.4 5.6 fusion.8
  264.1 5.6 fusion.159
  273.4 4.1 fusion.71
  277.6 4.2 fusion.68
  284.6 4.2 fusion.91
  295.7 4.0 convolution_convert_fusion
  315.2 23.8 %all-reduce.50 = (bf16[512]{0:T(512)(128)(2,1)S(1)}, bf16[512]{0:T(512)(128)(2,1)S(1)}, bf16[512]{0:T(512)(128)(2,1)S(1)}, bf16[512]{0:T(512)(128)(2,1)S(1)}, bf...) all-reduce(bf16[512]{0:T(512)(128)(2,1)S(1)} %copy-done.167, ...), channel_id=1, replica_groups=mesh['dp'=4,'fsdp'=8] {'fsdp'}, use_global_device_ids=true, to_apply=%add.31 | all-reduce | flops 12800 | bytes 51200
  339.7 12.4 %all-reduce.52 = (bf16[64]{0:T(256)(128)(2,1)S(1)}, bf16[64]{0:T(256)(128)(2,1)S(1)}, bf16[64]{0:T(256)(128)(2,1)S(1)}, bf16[64]{0:T(256)(128)(2,1)S(1)}, bf16[6...) all-reduce(bf16[64]{0:T(256)(128)(2,1)S(1)} %fusion.336, ...), channel_id=1, replica_groups=mesh['dp'=4,'fsdp'=8] {'dp'}, use_global_device_ids=true, to_apply=%region_66.67 | all-reduce | flops 768 | bytes 3072 | tf_op jit(solution)/shard_map/psum | solution.py:285
  366.3 42.7 %reduce-scatter.19.cloned.1.call-done = bf16[64,2048]{1,0:T(8,128)(2,1)} async-done(((bf16[512,2048]{1,0:T(8,128)(2,1)}), bf16[64,2048]{1,0:T(8,128)(2,1)}) %reduce-scatter.19.cloned.1.call-update) | async-done | bytes 262160 | tf_op jit(solution)/shard_map/reduce_scatter | solution.py:270
  409.1 44.9 %reduce-scatter.17.cloned.1.call-done = bf16[64,2048]{1,0:T(8,128)(2,1)} async-done(((bf16[512,2048]{1,0:T(8,128)(2,1)}), bf16[64,2048]{1,0:T(8,128)(2,1)}) %reduce-scatter.17.cloned.1.call-update) | async-done | bytes 262160 | tf_op jit(solution)/shard_map/reduce_scatter | solution.py:270
  455.8 42.6 %reduce-scatter.23.cloned.1.call-done = bf16[256,512]{1,0:T(8,128)(2,1)} async-done(((bf16[2048,512]{1,0:T(8,128)(2,1)}), bf16[256,512]{1,0:T(8,128)(2,1)}) %reduce-scatter.23.cloned.1.call-update) | async-done | bytes 262160 | tf_op jit(solution)/shard_map/reduce_scatter | solution.py:276
  498.3 44.9 %reduce-scatter.21.cloned.1.call-done = bf16[256,512]{1,0:T(8,128)(2,1)} async-done(((bf16[2048,512]{1,0:T(8,128)(2,1)}), bf16[256,512]{1,0:T(8,128)(2,1)}) %reduce-scatter.21.cloned.1.call-update) | async-done | bytes 262160 | tf_op jit(solution)/shard_map/reduce_scatter | solution.py:276
  550.1 41.4 %all-reduce.56.cloned.1.call-done = (bf16[64,1536]{1,0:T(8,128)(2,1)}, bf16[64,512]{1,0:T(8,128)(2,1)}, bf16[64,2048]{1,0:T(8,128)(2,1)}, bf16[256,512]{1,0:T(8,128)(2,1)}) async-done(((bf16[64,1536]{1,0:T(8,128)(2,1)}, bf16[64,512]{1,0:T(8,128)(2,1)}, bf16[64,2048]{1,0:T(8,128)(2,1)}, bf16[256,512]{1,0:T(8,128)(2,1)}), (bf16[64,1536]{1,0:T(8,128)(2,1)}, bf16[64,512]{1,0:T(8,128)(2,1)}, ...) | async-done | bytes 786448 | tf_op jit(solution)/shard_map/psum | solution.py:287
  (645 shorter events, 210.6 us)
Async XLA Ops:
  7.2 52.8 %copy-start.2 = (bf16[2,1,384,512]{3,2,1,0:T(8,128)(2,1)S(1)}, bf16[2,1,384,512]{3,2,1,0:T(8,128)(2,1)}, u32[]{:S(2)}) copy-start(bf16[2,1,384,512]{3,2,1,0:T(8,128)(2,1)} %param.28) | copy-start | bytes 2359300
  7.2 54.8 %all-gather.5.cloned.1.call-start = ((), (), s32[]{:S(2)}) async-start(), calls=%async_computation.8 | async-start | bytes 1769472 | tf_op jit(solution)/shard_map/all_gather | solution.py:210
  7.9 99.0 %all-gather.9.cloned.1.call-start = ((), (), s32[]{:S(2)}) async-start(), calls=%async_computation.10 | async-start | bytes 2359296 | tf_op jit(solution)/shard_map/all_gather | solution.py:219
  8.7 104.4 %all-gather.7.cloned.1.call-start = ((), (), s32[]{:S(2)}) async-start(), calls=%async_computation.9 | async-start | bytes 2359296 | tf_op jit(solution)/shard_map/all_gather | solution.py:217
  9.4 352.7 %reduce-scatter.15.cloned.1.call-start = ((), (), s32[]{:S(2)}) async-start(), calls=%async_computation.14 | async-start | bytes 589824 | tf_op jit(solution)/shard_map/reduce_scatter | solution.py:258
  10.9 51.0 %copy-start.135 = (s32[1,384]{1,0:T(1,128)}, s32[1,384]{1,0:T(1,128)S(1)}, u32[]{:S(2)}) copy-start(s32[1,384]{1,0:T(1,128)S(1)} %reshape.4314) | copy-start | bytes 4612
  11.1 50.8 %copy-start.137 = (s32[1,384]{1,0:T(1,128)}, s32[1,384]{1,0:T(1,128)S(1)}, u32[]{:S(2)}) copy-start(s32[1,384]{1,0:T(1,128)S(1)} %reshape.4310) | copy-start | bytes 4612
  35.5 25.9 %copy-start.96 = (f32[512]{0:T(512)}, f32[512]{0:T(512)S(1)}, u32[]{:S(2)}) copy-start(f32[512]{0:T(512)S(1)} %convert_element_type.980) | copy-start | bytes 6148
  39.1 22.3 %copy-start.100 = (f32[384]{0:T(512)}, f32[384]{0:T(512)S(1)}, u32[]{:S(2)}) copy-start(f32[384]{0:T(512)S(1)} %broadcast_multiply_fusion.3) | copy-start | bytes 4612
  39.1 22.3 %copy-start.98 = (f32[384]{0:T(512)}, f32[384]{0:T(512)S(1)}, u32[]{:S(2)}) copy-start(f32[384]{0:T(512)S(1)} %broadcast_multiply_fusion.1) | copy-start | bytes 4612
  60.0 41.8 %copy-start.11 = (bf16[512,512]{1,0:T(8,128)(2,1)}, bf16[512,512]{1,0:T(8,128)(2,1)S(1)}, u32[]{:S(2)}) copy-start(bf16[512,512]{1,0:T(8,128)(2,1)S(1)} %all_gather.31) | copy-start | bytes 1572868
  102.2 26.6 %copy-start.7 = (f32[384,512]{1,0:T(8,128)}, f32[384,512]{1,0:T(8,128)S(1)}, u32[]{:S(2)}) copy-start(f32[384,512]{1,0:T(8,128)S(1)} %get-tuple-element.809) | copy-start | bytes 2359300
  104.3 24.6 %copy-start.9 = (f32[384,512]{1,0:T(8,128)}, f32[384,512]{1,0:T(8,128)S(1)}, u32[]{:S(2)}) copy-start(f32[384,512]{1,0:T(8,128)S(1)} %get-tuple-element.811) | copy-start | bytes 2359300
  145.6 216.5 %reduce-scatter.13.cloned.1.call-start = ((), (), s32[]{:S(2)}) async-start(), calls=%async_computation.13 | async-start | bytes 589824 | tf_op jit(solution)/shard_map/reduce_scatter | solution.py:258
  246.6 117.1 %reduce-scatter.11.cloned.1.call-start = ((), (), s32[]{:S(2)}) async-start(), calls=%async_computation.12 | async-start | bytes 1769472 | tf_op jit(solution)/shard_map/reduce_scatter | solution.py:249
  253.6 110.9 %reduce-scatter.9.cloned.1.call-start = ((), (), s32[]{:S(2)}) async-start(), calls=%async_computation.11 | async-start | bytes 1769472 | tf_op jit(solution)/shard_map/reduce_scatter | solution.py:249
  273.3 135.8 %reduce-scatter.19.cloned.1.call-start = ((), (), s32[]{:S(2)}) async-start(), calls=%async_computation.16 | async-start | bytes 2359296 | tf_op jit(solution)/shard_map/reduce_scatter | solution.py:270
  277.5 176.5 %reduce-scatter.17.cloned.1.call-start = ((), (), s32[]{:S(2)}) async-start(), calls=%async_computation.15 | async-start | bytes 2359296 | tf_op jit(solution)/shard_map/reduce_scatter | solution.py:270
  281.8 216.6 %reduce-scatter.23.cloned.1.call-start = ((), (), s32[]{:S(2)}) async-start(), calls=%async_computation.18 | async-start | bytes 2359296 | tf_op jit(solution)/shard_map/reduce_scatter | solution.py:276
  299.8 243.4 %reduce-scatter.21.cloned.1.call-start = ((), (), s32[]{:S(2)}) async-start(), calls=%async_computation.17 | async-start | bytes 2359296 | tf_op jit(solution)/shard_map/reduce_scatter | solution.py:276
  312.3 44.5 %copy-start.10 = (f32[384,512]{1,0:T(8,128)S(1)}, f32[384,512]{1,0:T(8,128)}, u32[]{:S(2)}) copy-start(f32[384,512]{1,0:T(8,128)} %copy-done.9) | copy-start | bytes 2359300
  315.0 276.5 %all-reduce.56.cloned.1.call-start = ((), (), s32[]{:S(2)}) async-start(), calls=%async_computation.19 | async-start | bytes 1572864 | tf_op jit(solution)/shard_map/psum | solution.py:287
  362.1 185.7 %copy-start.31 = (f32[384,512]{1,0:T(8,128)S(1)}, f32[384,512]{1,0:T(8,128)}, u32[]{:S(2)}) copy-start(f32[384,512]{1,0:T(8,128)} %copy-done.30) | copy-start | bytes 2359300
  362.1 185.7 %copy-start.115 = (f32[384]{0:T(512)S(1)}, f32[384]{0:T(512)}, u32[]{:S(2)}) copy-start(f32[384]{0:T(512)} %copy-done.113) | copy-start | bytes 4612
  (167 other events, 835.7 us)
Sparse Core Ops, SparseCore 0:
  9.9 28.5 all-gather.4
  40.3 27.9 all-gather.8
  70.2 27.8 all-gather.6
  145.8 34.2 reduce-scatter.14
  246.7 34.2 reduce-scatter.12
  284.2 38.5 reduce-scatter.10
  326.0 38.4 reduce-scatter.8
  367.9 41.1 reduce-scatter.18
  412.7 41.2 reduce-scatter.16
  457.1 41.1 reduce-scatter.22
  502.0 41.2 reduce-scatter.20
  546.9 44.6 all-reduce.55
where the time goes:
time: 611 us; the launch traced here: 605 us
  waiting for transfers between devices  220 us (36%)
  matrix products  133 us (22%)
  other arithmetic  106 us (17%)
  blocking collectives  69.9 us (11%)
  local copies, waits for them, and re-layouts  56.8 us (9%)
  between operations  19 us (3%)
    reduce_scatter x2, waiting for transfers between devices, shards(): lax.psum_scatter(grad_w[9].astype(jnp.bfloat16), 'fsdp', scatter_dimensio...  87.6 us
    reduce_scatter x2, waiting for transfers between devices, shards(): lax.psum_scatter(grad_w[11].astype(jnp.bfloat16), 'fsdp', scatter_dimensi...  87.5 us
    dot_general x30, matrix products, matmul(): return jnp.dot(left, right, preferred_element_type=jnp.float32)  67.6 us
    psum x1, waiting for transfers between devices, shards(): lax.psum(shares[2].astype(jnp.bfloat16), 'dp').astype(jnp.float32)  41.4 us
    unnamed x2, blocking collectives  39.5 us
    dot_general x8, matrix products, one_block(): jnp.einsum('qhd,khd->hqk', query_tile, k_block, preferred_element_type=jn...  32.8 us
    dot_general x6, matrix products, one_block(): jnp.einsum('hqk,khd->qhd', p_frames, v_block, preferred_element_type=jnp....  21 us
    reduce_sum x1, other arithmetic, one_block(): e_frames = jnp.exp(s_frames - top)  17.4 us
  transfers between devices with their start and end apart: 12, of which 6 were waited for; matrix products, arithmetic and copies ran while one was open for 41% of the time, Pallas kernels for 0%

commit v1 on v0

v1 whole, which is shorter than its diff:
```python
import functools

import jax
import jax.numpy as jnp
from jax import lax
from jax.experimental import pallas as pl
from jax.experimental.pallas import tpu as pltpu
from jax.sharding import PartitionSpec as P

HEADS = 8
SEG = 16
RIGHT = 4
LEFT = 30
MEMS = 4
QB = 128
WIN = 176
SLOTS = 16
KEYS = WIN + SLOTS
TILE = 512
EXTRA = 16
BF = jnp.bfloat16
F32 = jnp.float32
HBM = pl.BlockSpec(memory_space=pl.ANY)
VMEM = pl.BlockSpec(memory_space=pltpu.VMEM)
LIMIT = 56 * 2**20


def nn(a, b):
    return lax.dot_general(a, b, (((1,), (0,)), ((), ())), preferred_element_type=F32)


def nt(a, b):
    return lax.dot_general(a, b, (((1,), (1,)), ((), ())), preferred_element_type=F32)


def tn(a, b):
    return lax.dot_general(a, b, (((0,), (0,)), ((), ())), preferred_element_type=F32)


def params(**more):
    return pltpu.CompilerParams(vmem_limit_bytes=LIMIT, **more)


def window(block, length):
    first = min(max(block * QB - 32, 0), length - WIN)
    slot = min(max(block * QB // SEG - MEMS, 0), length // SEG - SLOTS)
    return first, slot


def pieces_of(parts, width):
    plan = []
    for number, (offset, relative, first, rows, count) in enumerate(parts):
        for each in range(count):
            plan.append((number, each * rows, rows, offset + each, relative, first))
    return plan


def start_copies(copies):
    for copy in copies:
        copy.start()


def wait_copies(copies):
    for copy in copies:
        copy.wait()


def stats(value):
    mean = jnp.mean(value, axis=-1, keepdims=True)
    offset = value - mean
    spread = jnp.mean(offset * offset, axis=-1, keepdims=True)
    scale = lax.rsqrt(spread + 1e-05)
    return offset * scale, scale


def averages(length):
    blocks = length // QB
    rows = blocks * SLOTS
    row = lax.broadcasted_iota(jnp.int32, (rows, length), 0)
    seg = lax.broadcasted_iota(jnp.int32, (rows, length), 1) // SEG
    slot = row % SLOTS
    for block in range(blocks):
        first = window(block, length)[1]
        slot = slot + jnp.where(row // SLOTS == block, first, 0)
    return jnp.where(slot == seg, 1.0 / SEG, 0.0).astype(BF)


def head_pair(value):
    lane = lax.broadcasted_iota(jnp.int32, value.shape, 1)
    zero = jnp.zeros_like(value)
    half = value.shape[1] // 2
    return jnp.concatenate(
        [jnp.where(lane < half, value, zero), jnp.where(lane >= half, value, zero)], axis=0
    )


def diagonal(value):
    half = value.shape[0] // 2
    return jnp.concatenate([value[:half, :QB], value[half:, QB:]], axis=0)


def visible_bias(bias_ref, utter_ref, row, nsegs):
    length = nsegs * SEG
    key = lax.broadcasted_iota(jnp.int32, (KEYS, QB), 0)
    query = lax.broadcasted_iota(jnp.int32, (KEYS, QB), 1)
    segs = QB // SEG
    starts = [jnp.int32(0)]
    for seg in range(1, nsegs):
        same = utter_ref[row, seg] == utter_ref[row, seg - 1]
        starts.append(jnp.where(same, starts[-1], seg))
    for block in range(length // QB):
        first, slot = window(block, length)
        lower = jnp.zeros((KEYS, QB), jnp.int32)
        upper = jnp.zeros((KEYS, QB), jnp.int32)
        for part in range(segs):
            seg = block * segs + part
            more = jnp.int32(0)
            if seg + 1 < nsegs:
                more = jnp.where(utter_ref[row, seg + 1] == utter_ref[row, seg], RIGHT, 0)
            frame_low = jnp.maximum(seg * SEG - LEFT, starts[seg] * SEG) - first
            frame_high = seg * SEG + SEG + more - first
            slot_low = jnp.maximum(seg - MEMS, starts[seg]) - slot + WIN
            slot_high = jnp.int32(seg - slot + WIN)
            here = query // SEG == part
            lower = jnp.where(here, jnp.where(key < WIN, frame_low, slot_low), lower)
            upper = jnp.where(here, jnp.where(key < WIN, frame_high, slot_high), upper)
        seen = (key >= lower) & (key < upper)
        bias_ref[block] = jnp.where(seen, 0.0, -1e9)


def front_body(plan, width, nparts, utter, x, *refs):
    parts = refs[:nparts]
    (vecs, q_out, k_out, v_out, p_out, att_out, resid_out, n2_out) = refs[nparts : nparts + 8]
    (w_in, w_out, small, bias, att, sem) = refs[nparts + 8 :]
    row = pl.program_id(0)
    length, model = x.shape[1], x.shape[2]
    pieces = small.shape[0]
    blocks = length // QB
    me = lax.axis_index("fsdp")

    @pl.when(row == 0)
    def _():
        copies = []
        for number, at, rows, offset, relative, first in plan:
            device = jnp.bitwise_xor(me, offset) if relative else offset
            for band in range(5):
                low, high = band * width, (band + 1) * width if band < 4 else 4 * width + EXTRA
                low, high = max(low, first), min(high, first + rows)
                if low >= high:
                    continue
                source = parts[number].at[pl.ds(at + low - first, high - low), :]
                if band == 4:
                    target = small.at[device]
                else:
                    place = pl.multiple_of(device * width, width) + low - band * width
                    if band < 3:
                        target = w_in.at[pl.ds(place, high - low), pl.ds(band * model, model)]
                    else:
                        target = w_out.at[pl.ds(place, high - low), :]
                copies.append(pltpu.make_async_copy(source, target, sem))
        start_copies(copies)
        wait_copies(copies)
        total = jnp.zeros((8, model), F32)
        ups = [jnp.zeros((1, model), F32) for _ in range(4)]
        for piece in range(pieces):
            found = small[piece].astype(F32)
            total = total + pltpu.roll(found, piece * width, 1)[:8]
            for part in range(4):
                place = (piece * 4 + part) * width
                ups[place // model] += pltpu.roll(found, place % model, 1)[8 + part : 9 + part]
        vecs[0:8] = total
        for part in range(4):
            vecs[8 + part : 9 + part] = ups[part]
        vecs[12:16] = jnp.zeros((4, model), F32)

    visible_bias(bias, utter, row, length // SEG)
    value = x[0].astype(F32)
    unit, _ = stats(value)
    normed = (unit * vecs[0:1] + vecs[1:2]).astype(BF)
    summary = nn(averages(length), normed).astype(BF)
    wide = jnp.concatenate([normed, summary], axis=0)
    q_out[0] = ((nn(normed, w_in[:, :model]) + vecs[2:3]).astype(BF).astype(F32) * 0.125).astype(BF)
    k_out[0] = nn(wide, w_in[:, model : 2 * model]).astype(BF)
    v_out[0] = (nn(wide, w_in[:, 2 * model :]) + vecs[3:4]).astype(BF)
    for block in range(blocks):
        first, _ = window(block, length)
        rows = slice(block * QB, (block + 1) * QB)
        own = slice(length + block * SLOTS, length + (block + 1) * SLOTS)
        for pair in range(HEADS // 2):
            lanes = slice(pair * 128, (pair + 1) * 128)
            keys = jnp.concatenate([k_out[0, first : first + WIN, lanes], k_out[0, own, lanes]], axis=0)
            vals = jnp.concatenate([v_out[0, first : first + WIN, lanes], v_out[0, own, lanes]], axis=0)
            seen = bias[block]
            scores = nt(keys, head_pair(q_out[0, rows, lanes]))
            scores = scores + jnp.concatenate([seen, seen], axis=1)
            top = jnp.max(scores, axis=0, keepdims=True)
            raised = jnp.exp(scores - top)
            probs = (raised * (1.0 / jnp.sum(raised, axis=0, keepdims=True))).astype(BF)
            p_out[0, block, pair] = probs
            found = diagonal(tn(vals, probs))
            att_out[0, lanes, rows] = found.astype(BF)
            att[rows, lanes] = found.T.astype(BF)
    resid = value + nn(att[...], w_out[...]) + vecs[4:5]
    resid_out[0] = resid
    unit, _ = stats(resid)
    n2_out[0] = (unit * vecs[5:6] + vecs[6:7]).astype(BF)


def front(x, utter, parts, plan, width, pieces):
    rows, length, model = x.shape
    blocks = length // QB
    wide = length + blocks * SLOTS
    body = functools.partial(front_body, plan, width, len(parts))

    def by_row(*shape):
        zeros = (0,) * len(shape)
        return pl.BlockSpec((1,) + shape, lambda r, *_: (r,) + zeros)

    return pl.pallas_call(
        body,
        grid=(rows,),
        in_specs=[pl.BlockSpec(memory_space=pltpu.SMEM), by_row(length, model)] + [HBM] * len(parts),
        out_specs=[
            pl.BlockSpec((16, model), lambda r: (0, 0)),
            by_row(length, model),
            by_row(wide, model),
            by_row(wide, model),
            by_row(blocks, HEADS // 2, KEYS, 2 * QB),
            by_row(model, length),
            by_row(length, model),
            by_row(length, model),
        ],
        out_shape=[
            jax.ShapeDtypeStruct((16, model), F32),
            jax.ShapeDtypeStruct((rows, length, model), BF),
            jax.ShapeDtypeStruct((rows, wide, model), BF),
            jax.ShapeDtypeStruct((rows, wide, model), BF),
            jax.ShapeDtypeStruct((rows, blocks, HEADS // 2, KEYS, 2 * QB), BF),
            jax.ShapeDtypeStruct((rows, model, length), BF),
            jax.ShapeDtypeStruct((rows, length, model), F32),
            jax.ShapeDtypeStruct((rows, length, model), BF),
        ],
        scratch_shapes=[
            pltpu.VMEM((model, 3 * model), BF),
            pltpu.VMEM((model, model), BF),
            pltpu.VMEM((pieces, EXTRA, model), BF),
            pltpu.VMEM((blocks, KEYS, QB), F32),
            pltpu.VMEM((length, model), BF),
            pltpu.SemaphoreType.DMA,
        ],
        compiler_params=params(),
        name="front",
    )(utter, x, *parts)


def assemble(plan, parts, target, height, sem):
    me = lax.axis_index("fsdp")
    copies = []
    for number, at, rows, offset, relative, first in plan:
        device = jnp.bitwise_xor(me, offset) if relative else offset
        place = pl.multiple_of(device * height, height) + first
        copies.append(
            pltpu.make_async_copy(
                parts[number].at[pl.ds(at, rows), :], target.at[pl.ds(place, rows), :], sem
            )
        )
    return copies


def gelu_both(v):
    c = 0.7978845608028654
    square = v * v
    bent = jnp.tanh(c * v * (1.0 + 0.044715 * square))
    half = 0.5 + 0.5 * bent
    slope = half + 0.5 * v * (1.0 - bent * bent) * (c * (1.0 + 3 * 0.044715 * square))
    return v * half, slope


def middle_body(up_plan, down_plan, n_up, n_down, n2, dy, vecs, *refs):
    up_parts = refs[:n_up]
    down_parts = refs[n_up : n_up + n_down]
    hidden, du, grad, ub = refs[n_up + n_down : n_up + n_down + 4]
    up, down, dyt, sem = refs[n_up + n_down + 4 :]
    model = n2.shape[1]
    tokens = n2.shape[0]
    pieces = up.shape[0] // up_plan[1]
    copies = assemble(up_plan[0], up_parts, up, up_plan[1], sem.at[0])
    later = assemble(down_plan[0], down_parts, down, down_plan[1], sem.at[1])
    start_copies(copies)
    start_copies(later)
    dyt[...] = dy[...].T
    wait_copies(copies)
    wait_copies(later)
    step = 128
    for tile in range(up.shape[1] // TILE):
        cols = slice(tile * TILE, (tile + 1) * TILE)
        sums = jnp.zeros((1, TILE), F32)
        for chunk in range(tokens // step):
            rows = slice(chunk * step, (chunk + 1) * step)
            u = nn(n2[rows], up[:, cols]) + vecs[8 + tile : 9 + tile]
            value, slope = gelu_both(u)
            hidden[rows, cols] = value.astype(BF)
            back = nt(dy[rows], down[cols]).astype(BF).astype(F32) * slope
            du[rows, cols] = back.astype(BF)
            sums = sums + jnp.sum(back, axis=0, keepdims=True)
        ub[tile : tile + 1] = sums
        grad[:, cols] = nn(dyt[...], hidden[:, cols]).astype(BF)


def middle(n2, dy, vecs, up_parts, up_plan, down_parts, down_plan):
    tokens, model = n2.shape
    ff = up_parts[0].shape[1]
    body = functools.partial(middle_body, up_plan, down_plan, len(up_parts), len(down_parts))
    return pl.pallas_call(
        body,
        in_specs=[VMEM] * 3 + [HBM] * (len(up_parts) + len(down_parts)),
        out_specs=[VMEM] * 4,
        out_shape=[
            jax.ShapeDtypeStruct((tokens, ff), BF),
            jax.ShapeDtypeStruct((tokens, ff), BF),
            jax.ShapeDtypeStruct((model, ff), BF),
            jax.ShapeDtypeStruct((ff // TILE, TILE), F32),
        ],
        scratch_shapes=[
            pltpu.VMEM((model, ff), BF),
            pltpu.VMEM((ff, model), BF),
            pltpu.VMEM((model, tokens), BF),
            pltpu.SemaphoreType.DMA((2,)),
        ],
        compiler_params=params(),
        name="middle",
    )(n2, dy, vecs, *up_parts, *down_parts)


def norm_back(grad, unit, scale):
    first = jnp.mean(grad, axis=-1, keepdims=True)
    second = jnp.mean(grad * unit, axis=-1, keepdims=True)
    return scale * (grad - first - unit * second)


def back_body(up_plan, n_up, out_plan, width, n_out, n2, du, resid, dy, att, vecs, *refs):
    up_parts = refs[:n_up]
    out_parts = refs[n_up : n_up + n_out]
    gup, gout, dresid, datt, sums = refs[n_up + n_out : n_up + n_out + 5]
    up, w_out, n2t, sem = refs[n_up + n_out + 5 :]
    me = lax.axis_index("fsdp")
    tokens, model = n2.shape
    copies = assemble(up_plan[0], up_parts, up, up_plan[1], sem)
    for number, at, rows, offset, relative, first in out_plan:
        low, high = max(first, 3 * width), min(first + rows, 4 * width)
        if low < high:
            device = jnp.bitwise_xor(me, offset) if relative else offset
            place = pl.multiple_of(device * width, width) + low - 3 * width
            copies.append(
                pltpu.make_async_copy(
                    out_parts[number].at[pl.ds(at + low - first, high - low), :],
                    w_out.at[pl.ds(place, high - low), :],
                    sem,
                )
            )
    start_copies(copies)
    n2t[...] = n2[...].T
    for tile in range(du.shape[1] // TILE):
        cols = slice(tile * TILE, (tile + 1) * TILE)
        gup[:, cols] = nn(n2t[...], du[:, cols]).astype(BF)
    wait_copies(copies)
    step = 128
    per_row = att.shape[2] // step
    gains = jnp.zeros((1, model), F32)
    shifts = jnp.zeros((1, model), F32)
    biases = jnp.zeros((1, model), F32)
    downs = jnp.zeros((1, model), F32)
    for chunk in range(tokens // step):
        rows = slice(chunk * step, (chunk + 1) * step)
        grad = nt(du[rows], up[...])
        unit, scale = stats(resid[rows])
        gains = gains + jnp.sum(grad * unit, axis=0, keepdims=True)
        shifts = shifts + jnp.sum(grad, axis=0, keepdims=True)
        top = dy[rows].astype(F32)
        downs = downs + jnp.sum(top, axis=0, keepdims=True)
        total = top + norm_back(grad * vecs[5:6], unit, scale)
        biases = biases + jnp.sum(total, axis=0, keepdims=True)
        dresid[rows] = total
        datt[rows] = nt(total.astype(BF), w_out[...]).astype(BF)
    full = jnp.zeros((model, model), F32)
    length = att.shape[2]
    for row in range(att.shape[0]):
        rows = slice(row * length, (row + 1) * length)
        full = full + nn(att[row], dresid[rows].astype(BF))
    gout[...] = full.astype(BF)
    sums[0:1] = gains
    sums[1:2] = shifts
    sums[2:3] = biases
    sums[3:4] = downs


def back(n2, du, resid, dy, att, vecs, up_parts, up_plan, out_parts, out_plan, width):
    tokens, model = n2.shape
    ff = du.shape[1]
    body = functools.partial(back_body, up_plan, len(up_parts), out_plan, width, len(out_parts))
    return pl.pallas_call(
        body,
        in_specs=[VMEM] * 6 + [HBM] * (len(up_parts) + len(out_parts)),
        out_specs=[VMEM] * 5,
        out_shape=[
            jax.ShapeDtypeStruct((model, ff), BF),
            jax.ShapeDtypeStruct((model, model), BF),
            jax.ShapeDtypeStruct((tokens, model), F32),
            jax.ShapeDtypeStruct((tokens, model), BF),
            jax.ShapeDtypeStruct((4, model), F32),
        ],
        scratch_shapes=[
            pltpu.VMEM((model, ff), BF),
            pltpu.VMEM((model, model), BF),
            pltpu.VMEM((model, tokens), BF),
            pltpu.SemaphoreType.DMA,
        ],
        compiler_params=params(),
        name="back",
    )(n2, du, resid, dy, att, vecs, *up_parts, *out_parts)


def rear_body(plan, width, nparts, q, k, v, p, datt, x, dresid, vecs, *refs):
    parts = refs[:nparts]
    gin, dx, sums = refs[nparts : nparts + 3]
    (w_in, wide_all, mixed_all, dk, dv, sem) = refs[nparts + 3 :]
    row = pl.program_id(0)
    count = pl.num_programs(0)
    length, model = x.shape[1], x.shape[2]
    extent = k.shape[1]
    blocks = length // QB
    me = lax.axis_index("fsdp")

    copies = []
    for number, at, rows, offset, relative, first in plan:
        device = jnp.bitwise_xor(me, offset) if relative else offset
        for band in range(3):
            low, high = max(band * width, first), min((band + 1) * width, first + rows)
            if low < high:
                place = pl.multiple_of(device * width, width) + low - band * width
                copies.append(
                    pltpu.make_async_copy(
                        parts[number].at[pl.ds(at + low - first, high - low), :],
                        w_in.at[pl.ds(place, high - low), pl.ds(band * model, model)],
                        sem,
                    )
                )

    @pl.when(row == 0)
    def _():
        start_copies(copies)

    base = pl.multiple_of(row * extent, extent)
    value = x[0].astype(F32)
    unit, scale = stats(value)
    normed = (unit * vecs[0:1] + vecs[1:2]).astype(BF)
    average = averages(length)
    wide_all[pl.ds(base, length), :] = normed
    wide_all[pl.ds(base + length, extent - length), :] = nn(average, normed).astype(BF)
    dk[...] = jnp.zeros_like(dk)
    dv[...] = jnp.zeros_like(dv)
    mixed_all[pl.ds(base + length, extent - length), 0:model] = jnp.zeros((extent - length, model), BF)
    for block in range(blocks):
        first, _ = window(block, length)
        rows = slice(block * QB, (block + 1) * QB)
        own = slice(length + block * SLOTS, length + (block + 1) * SLOTS)
        span = slice(first, first + WIN)
        for pair in range(HEADS // 2):
            lanes = slice(pair * 128, (pair + 1) * 128)
            keys = jnp.concatenate([k[0, span, lanes], k[0, own, lanes]], axis=0)
            vals = jnp.concatenate([v[0, span, lanes], v[0, own, lanes]], axis=0)
            queries = head_pair(q[0, rows, lanes])
            tops = head_pair(datt[0, rows, lanes])
            probs = p[0, block, pair]
            wides = probs.astype(F32)
            back = nt(vals, tops)
            inner = jnp.sum(wides * back, axis=0, keepdims=True)
            dscores = (wides * (back - inner)).astype(BF)
            gv = nn(probs, tops)
            gk = nn(dscores, queries)
            dv[span, lanes] += gv[:WIN]
            dv[own, lanes] = gv[WIN:]
            dk[span, lanes] += gk[:WIN]
            dk[own, lanes] = gk[WIN:]
            gq = diagonal(tn(keys, dscores)).T * 0.125
            mixed_all[pl.ds(base + block * QB, QB), lanes] = gq.astype(BF)
    mixed_all[pl.ds(base, extent), model : 2 * model] = dk[...].astype(BF)
    mixed_all[pl.ds(base, extent), 2 * model :] = dv[...].astype(BF)

    @pl.when(row == 0)
    def _():
        wait_copies(copies)

    grad = nt(mixed_all[pl.ds(base, extent), :], w_in[...])
    grad = grad[:length] + tn(average, grad[length:].astype(BF))
    add = jnp.concatenate(
        [
            jnp.sum(grad * unit, axis=0, keepdims=True),
            jnp.sum(grad, axis=0, keepdims=True),
            jnp.sum(mixed_all[pl.ds(base, length), 0:model].astype(F32), axis=0, keepdims=True),
            jnp.sum(mixed_all[pl.ds(base, extent), 2 * model :].astype(F32), axis=0, keepdims=True),
        ],
        axis=0,
    )

    @pl.when(row == 0)
    def _():
        sums[...] = add

    @pl.when(row > 0)
    def _():
        sums[...] += add

    dx[0] = dresid[0] + norm_back(grad * vecs[0:1], unit, scale)

    @pl.when(row == count - 1)
    def _():
        for tile in range(3):
            cols = slice(tile * model, (tile + 1) * model)
            gin[:, cols] = tn(wide_all[...], mixed_all[:, cols]).astype(BF)


def rear(q, k, v, p, datt, x, dresid, vecs, parts, plan, width):
    rows, length, model = x.shape
    extent = k.shape[1]
    blocks = length // QB
    body = functools.partial(rear_body, plan, width, len(parts))

    def by_row(*shape):
        zeros = (0,) * len(shape)
        return pl.BlockSpec((1,) + shape, lambda r: (r,) + zeros)

    def whole(*shape):
        return pl.BlockSpec(shape, lambda r: (0,) * len(shape))

    return pl.pallas_call(
        body,
        grid=(rows,),
        in_specs=[
            by_row(length, model),
            by_row(extent, model),
            by_row(extent, model),
            by_row(blocks, HEADS // 2, KEYS, 2 * QB),
            by_row(length, model),
            by_row(length, model),
            by_row(length, model),
            whole(16, model),
        ]
        + [HBM] * len(parts),
        out_specs=[whole(model, 3 * model), by_row(length, model), whole(4, model)],
        out_shape=[
            jax.ShapeDtypeStruct((model, 3 * model), BF),
            jax.ShapeDtypeStruct((rows, length, model), F32),
            jax.ShapeDtypeStruct((4, model), F32),
        ],
        scratch_shapes=[
            pltpu.VMEM((model, 3 * model), BF),
            pltpu.VMEM((rows * extent, model), BF),
            pltpu.VMEM((rows * extent, 3 * model), BF),
            pltpu.VMEM((extent, model), F32),
            pltpu.VMEM((extent, model), F32),
            pltpu.SemaphoreType.DMA,
        ],
        compiler_params=params(),
        name="rear",
    )(q, k, v, p, datt, x, dresid, vecs, *parts)


def finish_body(plan, nparts, hidden, resid, vecs, *refs):
    parts = refs[:nparts]
    out, down, sem = refs[nparts:]
    copies = assemble(plan[0], parts, down, plan[1], sem)
    start_copies(copies)
    wait_copies(copies)
    step = 128
    for chunk in range(hidden.shape[0] // step):
        rows = slice(chunk * step, (chunk + 1) * step)
        out[rows] = (resid[rows] + nn(hidden[rows], down[...]) + vecs[7:8]).astype(BF)


def finish(hidden, resid, vecs, parts, plan):
    tokens, ff = hidden.shape
    model = resid.shape[1]
    return pl.pallas_call(
        functools.partial(finish_body, plan, len(parts)),
        in_specs=[VMEM] * 3 + [HBM] * len(parts),
        out_specs=VMEM,
        out_shape=jax.ShapeDtypeStruct((tokens, model), BF),
        scratch_shapes=[pltpu.VMEM((ff, model), BF), pltpu.SemaphoreType.DMA],
        compiler_params=params(),
        name="finish",
    )(hidden, resid, vecs, *parts)


def gather(piece, size):
    rows = piece.shape[0]
    whole = lax.all_gather(piece, "fsdp", axis=0, tiled=True)
    return [whole], pieces_of([(0, False, 0, rows, size)], rows)


def pack(project_in, project_out, vectors, up_bias):
    width, model = project_out.shape
    rows = jnp.concatenate(
        [jnp.stack(vectors), up_bias.reshape(4, width), jnp.zeros((4, width), BF)], axis=0
    )
    rows = jnp.pad(rows, ((0, 0), (0, model - width)))
    parts = [project_in[:, at * model : (at + 1) * model] for at in range(3)]
    return jnp.concatenate(parts + [project_out, rows], axis=0)


def scatter(value):
    own = lax.psum_scatter(value, "fsdp", scatter_dimension=0, tiled=True)
    return lax.psum(own, "dp").astype(F32)


def shards(
    frames,
    upstream,
    utterance,
    first_gain,
    first_shift,
    project_in,
    query_bias,
    value_bias,
    project_out,
    out_bias,
    second_gain,
    second_shift,
    up_weight,
    up_bias,
    down_weight,
    down_bias,
):
    micro, nrows, length, model = frames.shape
    rows = micro * nrows
    size = model // project_out.shape[0]
    width = model // size
    ff = up_weight.shape[1]
    x = frames.reshape(rows, length, model)
    dy = upstream.reshape(rows * length, model)
    utter = utterance.reshape(rows, length // SEG)
    vectors = (first_gain, first_shift, query_bias, value_bias, out_bias, second_gain, second_shift, down_bias)
    packed = pack(project_in, project_out, vectors, up_bias)
    a_parts, a_plan = gather(packed, size)
    u_parts, u_plan = gather(up_weight, size)
    d_parts, d_plan = gather(down_weight, size)
    vecs, q, k, v, p, att, resid, n2 = front(x, utter, a_parts, a_plan, width, size)
    n2 = n2.reshape(rows * length, model)
    flat = resid.reshape(rows * length, model)
    hidden, du, gdown, gub = middle(n2, dy, vecs, u_parts, (u_plan, width), d_parts, (d_plan, ff // size))
    gup, gout, dresid, datt, sums2 = back(
        n2, du, flat, dy, att, vecs, u_parts, (u_plan, width), a_parts, a_plan, width
    )
    shape = (rows, length, model)
    gin, dx, sums1 = rear(
        q, k, v, p, datt.reshape(shape), x, dresid.reshape(shape), vecs, a_parts, a_plan, width
    )
    out = finish(hidden, flat, vecs, d_parts, (d_plan, ff // size))
    small = jnp.concatenate([sums1, sums2, gub], axis=0)
    small = lax.psum(small, ("dp", "fsdp"))
    me = lax.axis_index("fsdp")

    def own(row):
        return lax.dynamic_slice_in_dim(small[row], me * width, width, 0)

    gub = lax.dynamic_slice_in_dim(small[8:].reshape(-1), me * (ff // size), ff // size, 0)
    return (
        out.reshape(frames.shape),
        dx.reshape(frames.shape),
        own(0),
        own(1),
        scatter(gin),
        own(2),
        own(3),
        scatter(gout),
        own(6),
        own(4),
        own(5),
        scatter(gup),
        gub,
        scatter(gdown.T),
        own(7),
    )


def solution(mesh):
    rows = P(None, ("dp", "fsdp"), None, None)
    vector = P("fsdp")
    matrix = P("fsdp", None)
    weights = (vector, vector, matrix, vector, vector, matrix, vector, vector, vector, matrix, vector, matrix, vector)
    return jax.shard_map(
        shards,
        mesh=mesh,
        in_specs=(rows, rows, P(None, ("dp", "fsdp"), None)) + weights,
        out_specs=(rows, rows) + weights,
        check_vma=False,
    )
```

time: 611 us -> 361 us (0.59)
  matrix products: 133 us -> 0 us
  other arithmetic: 106 us -> 4.99 us
  Pallas kernels: 0 us -> 67.7 us
  local copies, waits for them, and re-layouts: 56.8 us -> 10.6 us
  blocking collectives: 69.9 us -> 39.5 us
    dot_general x58 -> x0, matrix products: 133 us -> none  [the longest x30 67.6 us: matmul(): return jnp.dot(left, right, preferred_element_type=jnp.float32)]
    all_gather x3, waiting for transfers between devices: 0.02 us -> 75.1 us  [gather(): whole = lax.all_gather(piece, 'fsdp', axis=0, tiled=True)]
    reduce_scatter x8 -> x4, waiting for transfers between devices: 176 us -> 107 us  [scatter(): own = lax.psum_scatter(value, 'fsdp', scatter_dimension=0, tiled=True)]
    pallas_call x0 -> x5, Pallas kernels: none -> 67.7 us  [the longest x1 17.3 us: rear(): pl.pallas_call(body, grid=(rows,), in_specs=[by_row(length, model), by_ro...]
    reduce_sum x26 -> x0, other arithmetic: 44.3 us -> none  [the longest x1 17.4 us: one_block(): e_frames = jnp.exp(s_frames - top)]
    unnamed x2 -> x0, blocking collectives: 39.5 us -> none
    convert_element_type x53 -> x3, other arithmetic: 39.5 us -> 4.98 us  [scatter(): return lax.psum(own, 'dp').astype(F32)]
    psum x1, blocking collectives: 12.4 us -> 39.5 us  [shards(): small = lax.psum(small, ('dp', 'fsdp'))]
  transfers between devices with their start and end apart: 12 -> 8, of which waited for: 6 -> 7; matrix products, arithmetic and copies ran while one was open for 41% -> 1% of each run, Pallas kernels for 0% -> 11%
where the time goes in v1:
time: 361 us; the launch traced here: 360 us
  waiting for transfers between devices  223 us (62%)
  Pallas kernels  67.7 us (19%)
  blocking collectives  39.5 us (11%)
  between operations  14.3 us (4%)
  local copies, waits for them, and re-layouts  10.6 us (3%)
  other arithmetic  4.99 us (1%)
    reduce_scatter x4, waiting for transfers between devices, scatter(): own = lax.psum_scatter(value, 'fsdp', scatter_dimension=0, tiled=True)  107 us
    all_gather x3, waiting for transfers between devices, gather(): whole = lax.all_gather(piece, 'fsdp', axis=0, tiled=True)  75.1 us
    psum x1, blocking collectives, shards(): small = lax.psum(small, ('dp', 'fsdp'))  39.5 us
    psum x1, waiting for transfers between devices, scatter(): return lax.psum(own, 'dp').astype(F32)  37.9 us
    pallas_call x1, Pallas kernels, rear(): pl.pallas_call(body, grid=(rows,), in_specs=[by_row(length, model), by_ro...  17.3 us
    pallas_call x1, Pallas kernels, middle(): pl.pallas_call(body, in_specs=[VMEM] * 3 + [HBM] * (len(up_parts) + len(d...  16.2 us
    pallas_call x1, Pallas kernels, front(): pl.pallas_call(body, grid=(rows,), in_specs=[pl.BlockSpec(memory_space=pl...  14.3 us
    pallas_call x1, Pallas kernels, back(): pl.pallas_call(body, in_specs=[VMEM] * 6 + [HBM] * (len(up_parts) + len(o...  13.3 us
  transfers between devices with their start and end apart: 8, of which 7 were waited for; matrix products, arithmetic and copies ran while one was open for 1% of the time, Pallas kernels for 11%

profile of v1, /device:TPU:0, one launch (start us, length us, event | category | flops | bytes accessed | tf_op | source)
XLA Modules:
  0.0 360.4 jit_solution(8403225855147886433)
XLA Ops:
  7.2 0.8 slice_dynamic-update-slice_fusion.2
  8.1 0.8 slice_dynamic-update-slice_fusion.1
  8.9 0.8 slice_dynamic-update-slice_fusion
  9.8 0.7 reshape.73
  10.5 0.8 constant_dynamic-update-slice_fusion
  11.3 0.8 concatenate.9
  12.2 0.7 copy-done
  14.4 29.8 %all-gather.4.cloned.1.call-done.refs_0_.refs_1_ = bf16[2176,512]{1,0:T(8,128)(2,1)} async-done(((bf16[272,512]{1,0:T(8,128)(2,1)}), bf16[2176,512]{1,0:T(8,128)(2,1)}) %all-gather.4.cloned.1.call-update) | async-done | bytes 2228240 | tf_op jit(solution)/shard_map/all_gather | solution.py:597
  44.2 14.3 %front.1 = (f32[16,512]{1,0:T(8,128)}, bf16[2,384,512]{2,1,0:T(8,128)(2,1)}, bf16[2,432,512]{2,1,0:T(8,128)(2,1)}, bf16[2,432,512]{2,1,0:T(8,128)(2,1)}, bf16[2,...) custom-call(s32[2,24]{1,0:T(2,128)} %bitcast.54, ...), custom_call_target="tpu_custom_call" | custom-call | tf_op jit(solution)/shard_map/front/pallas_call | solution.py:219
  58.6 15.5 %all-gather.6.cloned.1.call-done.refs_0_ = bf16[512,2048]{1,0:T(8,128)(2,1)} async-done(((bf16[64,2048]{1,0:T(8,128)(2,1)}), bf16[512,2048]{1,0:T(8,128)(2,1)}) %all-gather.6.cloned.1.call-update) | async-done | bytes 2097168 | tf_op jit(solution)/shard_map/all_gather | solution.py:597
  74.1 29.8 %all-gather.8.cloned.1.call-done.refs_1_.refs_0_ = bf16[2048,512]{1,0:T(8,128)(2,1)} async-done(((bf16[256,512]{1,0:T(8,128)(2,1)}), bf16[2048,512]{1,0:T(8,128)(2,1)}) %all-gather.8.cloned.1.call-update) | async-done | bytes 2097168 | tf_op jit(solution)/shard_map/all_gather | solution.py:597
  103.9 16.2 %middle.1 = (bf16[768,2048]{1,0:T(8,128)(2,1)}, bf16[768,2048]{1,0:T(8,128)(2,1)}, bf16[512,2048]{1,0:T(8,128)(2,1)}, f32[4,512]{1,0:T(4,128)}) custom-call(bf16[768,512]{1,0:T(8,128)(2,1)} %bitcast.47, bf16[768,512]{1,0:T(8,128)(2,1)} %bitcast.45, f32[16,512]{1,0:T(8,128)} %get-tuple-element.36.vecs, ...), custom_call_target="tpu_custom_call" | custom-call | tf_op jit(solution)/shard_map/middle/pallas_call | solution.py:314
  120.1 13.3 %back.1 = (bf16[512,2048]{1,0:T(8,128)(2,1)}, bf16[512,512]{1,0:T(8,128)(2,1)}, f32[768,512]{1,0:T(8,128)}, bf16[768,512]{1,0:T(8,128)(2,1)}, f32[4,512]{1,0:T(4,128)}) custom-call(bf16[768,512]{1,0:T(8,128)(2,1)} %bitcast.48, bf16[768,2048]{1,0:T(8,128)(2,1)} %get-tuple-element.43.du, f32[768,512]{1,0:T(8,128)} %bitcast.41, bf16[768,512]{1,0:T(8,128)(2,1)} %bitcast.46, ...), custom_call_target="tpu_custom_call" | custom-call | tf_op jit(solution)/shard_map/back/pallas_call | solution.py:401
  133.5 17.3 %rear.1 = (bf16[512,1536]{1,0:T(8,128)(2,1)}, f32[2,384,512]{2,1,0:T(8,128)}, f32[4,512]{1,0:T(4,128)}) custom-call(bf16[2,384,512]{2,1,0:T(8,128)(2,1)} %get-tuple-element.39.q, bf16[2,432,512]{2,1,0:T(8,128)(2,1)} %get-tuple-element.40.k, bf16[2,432,512]{2,1,0:T(8,128)(2,1)} %get-tuple-element.41.v, bf16[2,3,4,192,256]{4,3,2,1,0:T(8,128)(2,1)} %get-tuple-element.42.p, ...), custom_call_target="tpu_custom_call" | custom-call | tf_op jit(solution)/shard_map/rear/pallas_call | solution.py:536
  152.3 39.5 %psum.35 = f32[12,512]{1,0:T(8,128)S(1)} all-reduce(f32[12,512]{1,0:T(8,128)S(1)} %pad_maximum_fusion), channel_id=1, replica_groups=mesh['dp'=4,'fsdp'=8] {'dp','fsdp'}, use_global_device_ids=true, to_apply=%region_0.1 | all-reduce | flops 6144 | bytes 49152 | tf_op jit(solution)/shard_map/psum | solution.py:660
  191.8 18.1 %reduce-scatter.5.cloned.1.call-done = bf16[64,1536]{1,0:T(8,128)(2,1)} async-done(((bf16[512,1536]{1,0:T(8,128)(2,1)}), bf16[64,1536]{1,0:T(8,128)(2,1)}) %reduce-scatter.5.cloned.1.call-update) | async-done | bytes 196624 | tf_op jit(solution)/shard_map/reduce_scatter | solution.py:612
  209.9 44.8 %reduce-scatter.11.cloned.1.call-done = bf16[256,512]{0,1:T(8,128)(2,1)} async-done(((bf16[2048,512]{0,1:T(8,128)(2,1)}), bf16[256,512]{0,1:T(8,128)(2,1)}) %reduce-scatter.11.cloned.1.call-update) | async-done | bytes 262160 | tf_op jit(solution)/shard_map/reduce_scatter | solution.py:612
  254.7 44.5 %reduce-scatter.9.cloned.1.call-done = bf16[64,2048]{1,0:T(8,128)(2,1)} async-done(((bf16[512,2048]{1,0:T(8,128)(2,1)}), bf16[64,2048]{1,0:T(8,128)(2,1)}) %reduce-scatter.9.cloned.1.call-update) | async-done | bytes 262160 | tf_op jit(solution)/shard_map/reduce_scatter | solution.py:612
  299.9 6.6 %finish.1 = bf16[768,512]{1,0:T(8,128)(2,1)} custom-call(bf16[768,2048]{1,0:T(8,128)(2,1)} %get-tuple-element.37.hidden, f32[768,512]{1,0:T(8,128)} %bitcast.42, f32[16,512]{1,0:T(8,128)} %get-tuple-element.36.vecs, bf16[2048,512]{1,0:T(8,128)(2,1)} %all-gather.8.cloned.1.call-done.refs_1_.refs_0_), custom_call_target="tpu_custom_call" | custom-call | tf_op jit(solution)/shard_map/finish/pallas_call | solution.py:584
  308.8 37.9 %all-reduce.4.cloned.1.call-done = (bf16[256,512]{0,1:T(8,128)(2,1)}, bf16[64,1536]{1,0:T(8,128)(2,1)}, bf16[64,512]{1,0:T(8,128)(2,1)}, bf16[64,2048]{1,0:T(8,128)(2,1)}) async-done(((bf16[256,512]{0,1:T(8,128)(2,1)}, bf16[64,1536]{1,0:T(8,128)(2,1)}, bf16[64,512]{1,0:T(8,128)(2,1)}, bf16[64,2048]{1,0:T(8,128)(2,1)}), (bf16[256,512]{0,1:T(8,128)(2,1)}, bf16[64,1536]{1,0:T(8,128)(2,1)}, ...) | async-done | bytes 786448 | tf_op jit(solution)/shard_map/psum | solution.py:613
  346.7 1.7 convert_element_type.14
  348.4 1.5 convert_element_type.15
  349.9 1.8 convert_element_type.16
  351.7 1.9 copy.33
  (35 shorter events, 6.0 us)
Async XLA Ops:
  7.2 37.0 %all-gather.4.cloned.1.call-start = ((), (), s32[]{:S(2)}) async-start(), calls=%async_computation.4 | async-start | bytes 2506752 | tf_op jit(solution)/shard_map/all_gather | solution.py:597
  12.2 0.7 copy-start
  12.9 61.1 %all-gather.6.cloned.1.call-start = ((), (), s32[]{:S(2)}) async-start(), calls=%async_computation.5 | async-start | bytes 2359296 | tf_op jit(solution)/shard_map/all_gather | solution.py:597
  13.7 90.2 %all-gather.8.cloned.1.call-start = ((), (), s32[]{:S(2)}) async-start(), calls=%async_computation.6 | async-start | bytes 2359296 | tf_op jit(solution)/shard_map/all_gather | solution.py:597
  14.4 177.4 %reduce-scatter.7.cloned.1.call-start = ((), (), s32[]{:S(2)}) async-start(), calls=%async_computation.8 | async-start | bytes 589824 | tf_op jit(solution)/shard_map/reduce_scatter | solution.py:612
  133.4 76.5 %reduce-scatter.5.cloned.1.call-start = ((), (), s32[]{:S(2)}) async-start(), calls=%async_computation.7 | async-start | bytes 1769472 | tf_op jit(solution)/shard_map/reduce_scatter | solution.py:612
  150.8 103.8 %reduce-scatter.11.cloned.1.call-start = ((), (), s32[]{:S(2)}) async-start(), calls=%async_computation.10 | async-start | bytes 2359296 | tf_op jit(solution)/shard_map/reduce_scatter | solution.py:612
  150.9 1.3 copy-start.1
  150.9 1.3 copy-start.2
  150.9 1.3 copy-start.3
  151.4 147.8 %reduce-scatter.9.cloned.1.call-start = ((), (), s32[]{:S(2)}) async-start(), calls=%async_computation.9 | async-start | bytes 2359296 | tf_op jit(solution)/shard_map/reduce_scatter | solution.py:612
  152.2 194.5 %all-reduce.4.cloned.1.call-start = ((), (), s32[]{:S(2)}) async-start(), calls=%async_computation.11 | async-start | bytes 1572864 | tf_op jit(solution)/shard_map/psum | solution.py:613
Sparse Core Ops, SparseCore 0:
  13.0 31.1 all-gather.3
  46.1 27.9 all-gather.5
  76.0 27.8 all-gather.7
  133.5 34.4 reduce-scatter.6
  171.5 38.3 reduce-scatter.4
  213.4 41.2 reduce-scatter.10
  257.9 41.1 reduce-scatter.8
  302.0 44.6 all-reduce.3

commit v2 on v1

--- a/solution.py
+++ b/solution.py
@@ -16,13 +16,14 @@
 WIN = 176
 SLOTS = 16
 KEYS = WIN + SLOTS
+SLOTS_OF = {(1, 0): 0, (3, 0): 1, (2, 1): 2, (3, 1): 3, (1, 1): 4, (2, 0): 5, (0, 0): 6, (0, 1): 7}
 TILE = 512
 EXTRA = 16
 BF = jnp.bfloat16
 F32 = jnp.float32
 HBM = pl.BlockSpec(memory_space=pl.ANY)
 VMEM = pl.BlockSpec(memory_space=pltpu.VMEM)
-LIMIT = 56 * 2**20
+LIMIT = 32 * 2**20
 
 
 def nn(a, b):
@@ -39,6 +40,10 @@
 
 def params(**more):
     return pltpu.CompilerParams(vmem_limit_bytes=LIMIT, **more)
+
+
+def cost(micros):
+    return pl.CostEstimate(flops=int(micros * 1.15e9), bytes_accessed=0, transcendentals=0)
 
 
 def window(block, length):
@@ -250,6 +255,7 @@
         ],
         compiler_params=params(),
         name="front",
+        cost_estimate=cost(14),
     )(utter, x, *parts)
 
 
@@ -267,6 +273,20 @@
     return copies
 
 
+def emit(full, grads, part, within, sem):
+    if len(grads) == 1:
+        return [pltpu.make_async_copy(full, within(grads[0]), sem)]
+    me = lax.axis_index("fsdp")
+    copies = []
+    for core in range(2):
+        for (chip, top), slot in SLOTS_OF.items():
+            device = jnp.bitwise_xor(me, 2 * chip + core)
+            copies.append(
+                pltpu.make_async_copy(part(device, top), within(grads[core].at[slot]), sem)
+            )
+    return copies
+
+
 def gelu_both(v):
     c = 0.7978845608028654
     square = v * v
@@ -276,11 +296,11 @@
     return v * half, slope
 
 
-def middle_body(up_plan, down_plan, n_up, n_down, n2, dy, vecs, *refs):
+def middle_body(up_plan, down_plan, n_up, n_down, n_grad, n2, dy, vecs, *refs):
     up_parts = refs[:n_up]
     down_parts = refs[n_up : n_up + n_down]
-    hidden, du, grad, ub = refs[n_up + n_down : n_up + n_down + 4]
-    up, down, dyt, sem = refs[n_up + n_down + 4 :]
+    hidden, du, ub, *grads = refs[n_up + n_down : n_up + n_down + 3 + n_grad]
+    up, down, dyt, grad, sem = refs[n_up + n_down + 3 + n_grad :]
     model = n2.shape[1]
     tokens = n2.shape[0]
     pieces = up.shape[0] // up_plan[1]
@@ -305,30 +325,45 @@
             sums = sums + jnp.sum(back, axis=0, keepdims=True)
         ub[tile : tile + 1] = sums
         grad[:, cols] = nn(dyt[...], hidden[:, cols]).astype(BF)
-
-
-def middle(n2, dy, vecs, up_parts, up_plan, down_parts, down_plan):
+    half = model // 2
+    copies = emit(
+        grad,
+        grads,
+        lambda device, top: grad.at[pl.ds(top * half, half), pl.ds(pl.multiple_of(device * down_plan[1], down_plan[1]), down_plan[1])],
+        lambda ref: ref,
+        sem.at[0],
+    )
+    start_copies(copies)
+    wait_copies(copies)
+
+
+def middle(n2, dy, vecs, up_parts, up_plan, down_parts, down_plan, fast):
     tokens, model = n2.shape
     ff = up_parts[0].shape[1]
-    body = functools.partial(middle_body, up_plan, down_plan, len(up_parts), len(down_parts))
+    shapes = [(8, model // 2, down_plan[1])] * 2 if fast else [(model, ff)]
+    body = functools.partial(
+        middle_body, up_plan, down_plan, len(up_parts), len(down_parts), len(shapes)
+    )
     return pl.pallas_call(
         body,
         in_specs=[VMEM] * 3 + [HBM] * (len(up_parts) + len(down_parts)),
-        out_specs=[VMEM] * 4,
+        out_specs=[VMEM] * 3 + [HBM] * len(shapes),
         out_shape=[
             jax.ShapeDtypeStruct((tokens, ff), BF),
             jax.ShapeDtypeStruct((tokens, ff), BF),
-            jax.ShapeDtypeStruct((model, ff), BF),
             jax.ShapeDtypeStruct((ff // TILE, TILE), F32),
-        ],
+        ]
+        + [jax.ShapeDtypeStruct(shape, BF) for shape in shapes],
         scratch_shapes=[
             pltpu.VMEM((model, ff), BF),
             pltpu.VMEM((ff, model), BF),
             pltpu.VMEM((model, tokens), BF),
+            pltpu.VMEM((model, ff), BF),
             pltpu.SemaphoreType.DMA((2,)),
         ],
         compiler_params=params(),
         name="middle",
+        cost_estimate=cost(16),
     )(n2, dy, vecs, *up_parts, *down_parts)
 
 
@@ -338,11 +373,11 @@
     return scale * (grad - first - unit * second)
 
 
-def back_body(up_plan, n_up, out_plan, width, n_out, n2, du, resid, dy, att, vecs, *refs):
+def back_body(up_plan, n_up, out_plan, width, n_out, n_grad, n2, du, resid, dy, att, vecs, *refs):
     up_parts = refs[:n_up]
     out_parts = refs[n_up : n_up + n_out]
-    gup, gout, dresid, datt, sums = refs[n_up + n_out : n_up + n_out + 5]
-    up, w_out, n2t, sem = refs[n_up + n_out + 5 :]
+    dresid, datt, sums, *grads = refs[n_up + n_out : n_up + n_out + 3 + n_grad]
+    up, w_out, n2t, gup, gout, sem = refs[n_up + n_out + 3 + n_grad :]
     me = lax.axis_index("fsdp")
     tokens, model = n2.shape
     copies = assemble(up_plan[0], up_parts, up, up_plan[1], sem)
@@ -388,42 +423,57 @@
         rows = slice(row * length, (row + 1) * length)
         full = full + nn(att[row], dresid[rows].astype(BF))
     gout[...] = full.astype(BF)
+    half = width // 2
+    ff = gup.shape[1]
+
+    def part_of(full):
+        return lambda device, top: full.at[pl.ds(pl.multiple_of(device * width, width) + top * half, half), :]
+
+    copies = emit(gup, grads, part_of(gup), lambda ref: ref.at[:, 0:ff], sem)
+    copies += emit(gout, grads, part_of(gout), lambda ref: ref.at[:, ff : ff + model], sem)
+    start_copies(copies)
+    wait_copies(copies)
     sums[0:1] = gains
     sums[1:2] = shifts
     sums[2:3] = biases
     sums[3:4] = downs
 
 
-def back(n2, du, resid, dy, att, vecs, up_parts, up_plan, out_parts, out_plan, width):
+def back(n2, du, resid, dy, att, vecs, up_parts, up_plan, out_parts, out_plan, width, fast):
     tokens, model = n2.shape
     ff = du.shape[1]
-    body = functools.partial(back_body, up_plan, len(up_parts), out_plan, width, len(out_parts))
+    shapes = [(8, width // 2, ff + model)] * 2 if fast else [(model, ff + model)]
+    body = functools.partial(
+        back_body, up_plan, len(up_parts), out_plan, width, len(out_parts), len(shapes)
+    )
     return pl.pallas_call(
         body,
         in_specs=[VMEM] * 6 + [HBM] * (len(up_parts) + len(out_parts)),
-        out_specs=[VMEM] * 5,
+        out_specs=[VMEM] * 3 + [HBM] * len(shapes),
         out_shape=[
-            jax.ShapeDtypeStruct((model, ff), BF),
-            jax.ShapeDtypeStruct((model, model), BF),
             jax.ShapeDtypeStruct((tokens, model), F32),
             jax.ShapeDtypeStruct((tokens, model), BF),
             jax.ShapeDtypeStruct((4, model), F32),
-        ],
+        ]
+        + [jax.ShapeDtypeStruct(shape, BF) for shape in shapes],
         scratch_shapes=[
             pltpu.VMEM((model, ff), BF),
             pltpu.VMEM((model, model), BF),
             pltpu.VMEM((model, tokens), BF),
+            pltpu.VMEM((model, ff), BF),
+            pltpu.VMEM((model, model), BF),
             pltpu.SemaphoreType.DMA,
         ],
         compiler_params=params(),
         name="back",
+        cost_estimate=cost(13),
     )(n2, du, resid, dy, att, vecs, *up_parts, *out_parts)
 
 
-def rear_body(plan, width, nparts, q, k, v, p, datt, x, dresid, vecs, *refs):
+def rear_body(plan, width, nparts, n_grad, q, k, v, p, datt, x, dresid, vecs, *refs):
     parts = refs[:nparts]
-    gin, dx, sums = refs[nparts : nparts + 3]
-    (w_in, wide_all, mixed_all, dk, dv, sem) = refs[nparts + 3 :]
+    dx, sums, *grads = refs[nparts : nparts + 2 + n_grad]
+    (w_in, wide_all, mixed_all, dk, dv, gin, sem) = refs[nparts + 2 + n_grad :]
     row = pl.program_id(0)
     count = pl.num_programs(0)
     length, model = x.shape[1], x.shape[2]
@@ -518,13 +568,24 @@
         for tile in range(3):
             cols = slice(tile * model, (tile + 1) * model)
             gin[:, cols] = tn(wide_all[...], mixed_all[:, cols]).astype(BF)
-
-
-def rear(q, k, v, p, datt, x, dresid, vecs, parts, plan, width):
+        half = width // 2
+        sends = emit(
+            gin,
+            grads,
+            lambda device, top: gin.at[pl.ds(pl.multiple_of(device * width, width) + top * half, half), :],
+            lambda ref: ref,
+            sem,
+        )
+        start_copies(sends)
+        wait_copies(sends)
+
+
+def rear(q, k, v, p, datt, x, dresid, vecs, parts, plan, width, fast):
     rows, length, model = x.shape
     extent = k.shape[1]
     blocks = length // QB
-    body = functools.partial(rear_body, plan, width, len(parts))
+    shapes = [(8, width // 2, 3 * model)] * 2 if fast else [(model, 3 * model)]
+    body = functools.partial(rear_body, plan, width, len(parts), len(shapes))
 
     def by_row(*shape):
         zeros = (0,) * len(shape)
@@ -547,22 +608,24 @@
             whole(16, model),
         ]
         + [HBM] * len(parts),
-        out_specs=[whole(model, 3 * model), by_row(length, model), whole(4, model)],
+        out_specs=[by_row(length, model), whole(4, model)] + [HBM] * len(shapes),
         out_shape=[
-            jax.ShapeDtypeStruct((model, 3 * model), BF),
             jax.ShapeDtypeStruct((rows, length, model), F32),
             jax.ShapeDtypeStruct((4, model), F32),
-        ],
+        ]
+        + [jax.ShapeDtypeStruct(shape, BF) for shape in shapes],
         scratch_shapes=[
             pltpu.VMEM((model, 3 * model), BF),
             pltpu.VMEM((rows * extent, model), BF),
             pltpu.VMEM((rows * extent, 3 * model), BF),
             pltpu.VMEM((extent, model), F32),
             pltpu.VMEM((extent, model), F32),
+            pltpu.VMEM((model, 3 * model), BF),
             pltpu.SemaphoreType.DMA,
         ],
         compiler_params=params(),
         name="rear",
+        cost_estimate=cost(17),
     )(q, k, v, p, datt, x, dresid, vecs, *parts)
 
 
@@ -589,31 +652,100 @@
         scratch_shapes=[pltpu.VMEM((ff, model), BF), pltpu.SemaphoreType.DMA],
         compiler_params=params(),
         name="finish",
+        cost_estimate=cost(6),
     )(hidden, resid, vecs, *parts)
 
 
-def gather(piece, size):
+def along(value, offset):
+    return lax.ppermute(value, "fsdp", [(i, i ^ offset) for i in range(8)])
+
+
+def across(value, offset, size):
+    return lax.ppermute(value, "dp", [(i, i ^ offset) for i in range(size)])
+
+
+def gather(piece, size, cut):
     rows = piece.shape[0]
-    whole = lax.all_gather(piece, "fsdp", axis=0, tiled=True)
-    return [whole], pieces_of([(0, False, 0, rows, size)], rows)
+    if size != 8:
+        whole = lax.all_gather(piece, "fsdp", axis=0, tiled=True)
+        return [whole], pieces_of([(0, False, 0, rows, size)], rows)
+    along_x = along(piece, 2)
+    along_y = along(piece, 4)
+    core = along(piece, 1)
+    top = along(along_x[:cut], 4)
+    bottom = along(along_y[cut:], 2)
+    parts = [piece, core, along_x, along_y]
+    parts += [along(along_x, 1), along(along_y, 1), top, bottom, along(top, 1), along(bottom, 1)]
+    whole = [(offset, True, 0, rows, 1) for offset in (0, 1, 2, 4, 3, 5)]
+    halves = [(offset, True, first, count, 1) for offset in (6, 7) for first, count in ((0, cut), (cut, rows - cut))]
+    return parts, pieces_of(whole + halves, rows)
+
+
+def pack_body(w_in, w_out, *refs):
+    vectors = refs[:8]
+    up_bias, out = refs[8:]
+    width, model = w_out.shape
+    for band in range(3):
+        out[band * width : (band + 1) * width] = w_in[:, band * model : (band + 1) * model]
+    out[3 * width : 4 * width] = w_out[...]
+    rows = [vector[...].astype(F32).reshape(1, width) for vector in vectors]
+    bias = up_bias[...].astype(F32).reshape(1, 4 * width)
+    rows += [bias[:, at * width : (at + 1) * width] for at in range(4)]
+    rows += [jnp.zeros((4, width), F32)]
+    out[4 * width :] = jnp.zeros((EXTRA, model), BF)
+    out[4 * width :, 0:width] = jnp.concatenate(rows, axis=0).astype(BF)
 
 
 def pack(project_in, project_out, vectors, up_bias):
     width, model = project_out.shape
-    rows = jnp.concatenate(
-        [jnp.stack(vectors), up_bias.reshape(4, width), jnp.zeros((4, width), BF)], axis=0
-    )
-    rows = jnp.pad(rows, ((0, 0), (0, model - width)))
-    parts = [project_in[:, at * model : (at + 1) * model] for at in range(3)]
-    return jnp.concatenate(parts + [project_out, rows], axis=0)
-
-
-def scatter(value):
-    own = lax.psum_scatter(value, "fsdp", scatter_dimension=0, tiled=True)
-    return lax.psum(own, "dp").astype(F32)
+    return pl.pallas_call(
+        pack_body,
+        in_specs=[VMEM] * 11,
+        out_specs=VMEM,
+        out_shape=jax.ShapeDtypeStruct((4 * width + EXTRA, model), BF),
+        compiler_params=params(),
+        name="pack",
+        cost_estimate=cost(3),
+    )(project_in, project_out, *vectors, up_bias)
+
+
+def plus(*values):
+    total = values[0].astype(F32)
+    for value in values[1:]:
+        total = total + value.astype(F32)
+    return total
+
+
+def scatter(grads, size, dims):
+    if len(grads) == 1:
+        own = lax.psum_scatter(grads[0], "fsdp", scatter_dimension=dims, tiled=True)
+        return lax.psum(own, "dp").astype(F32)
+    here, there = grads
+    held = plus(here, along(there, 1)).astype(BF)
+    from_x = along(held[0:2], 2)
+    from_y = along(held[2:4], 4)
+    next_x = along(plus(held[4], from_y[1]).astype(BF), 2)
+    next_y = along(plus(held[5], from_x[1]).astype(BF), 4)
+    top = plus(held[6], from_x[0], next_y).astype(BF)
+    bottom = plus(held[7], from_y[0], next_x).astype(BF)
+    own = jnp.stack([top, bottom])
+    own = plus(own, across(own, 1, size)).astype(BF)
+    own = plus(own, across(own, 2, size))
+    return own.reshape(-1, own.shape[2])
+
+
+def reduce_small(value, size, fast):
+    if not fast:
+        return lax.psum(value, ("dp", "fsdp"))
+    for offset in (1, 2, 4):
+        value = value + along(value, offset)
+    for offset in (1, 2):
+        value = value + across(value, offset, size)
+    return value
 
 
 def shards(
+    group,
     frames,
     upstream,
     utterance,
@@ -640,45 +772,51 @@
     dy = upstream.reshape(rows * length, model)
     utter = utterance.reshape(rows, length // SEG)
     vectors = (first_gain, first_shift, query_bias, value_bias, out_bias, second_gain, second_shift, down_bias)
+    fast = size == 8 and group == 4
     packed = pack(project_in, project_out, vectors, up_bias)
-    a_parts, a_plan = gather(packed, size)
-    u_parts, u_plan = gather(up_weight, size)
-    d_parts, d_plan = gather(down_weight, size)
+    a_parts, a_plan = gather(packed, size, 2 * width)
+    u_parts, u_plan = gather(up_weight, size, width // 2)
+    d_parts, d_plan = gather(down_weight, size, ff // size // 2)
     vecs, q, k, v, p, att, resid, n2 = front(x, utter, a_parts, a_plan, width, size)
     n2 = n2.reshape(rows * length, model)
     flat = resid.reshape(rows * length, model)
-    hidden, du, gdown, gub = middle(n2, dy, vecs, u_parts, (u_plan, width), d_parts, (d_plan, ff // size))
-    gup, gout, dresid, datt, sums2 = back(
-        n2, du, flat, dy, att, vecs, u_parts, (u_plan, width), a_parts, a_plan, width
+    hidden, du, gub, *gdown = middle(
+        n2, dy, vecs, u_parts, (u_plan, width), d_parts, (d_plan, ff // size), fast
+    )
+    dresid, datt, sums2, *gup = back(
+        n2, du, flat, dy, att, vecs, u_parts, (u_plan, width), a_parts, a_plan, width, fast
     )
     shape = (rows, length, model)
-    gin, dx, sums1 = rear(
-        q, k, v, p, datt.reshape(shape), x, dresid.reshape(shape), vecs, a_parts, a_plan, width
+    dx, sums1, *gin = rear(
+        q, k, v, p, datt.reshape(shape), x, dresid.reshape(shape), vecs, a_parts, a_plan, width, fast
     )
     out = finish(hidden, flat, vecs, d_parts, (d_plan, ff // size))
     small = jnp.concatenate([sums1, sums2, gub], axis=0)
-    small = lax.psum(small, ("dp", "fsdp"))
+    small = reduce_small(small, group, fast)
     me = lax.axis_index("fsdp")
 
     def own(row):
         return lax.dynamic_slice_in_dim(small[row], me * width, width, 0)
 
     gub = lax.dynamic_slice_in_dim(small[8:].reshape(-1), me * (ff // size), ff // size, 0)
+    gdown = scatter(gdown, group, 1).T
+    gup = scatter(gup, group, 0)
+    gin = scatter(gin, group, 0)
     return (
         out.reshape(frames.shape),
         dx.reshape(frames.shape),
         own(0),
         own(1),
-        scatter(gin),
+        gin,
         own(2),
         own(3),
-        scatter(gout),
+        gup[:, ff:],
         own(6),
         own(4),
         own(5),
-        scatter(gup),
+        gup[:, :ff],
         gub,
-        scatter(gdown.T),
+        gdown,
         own(7),
     )
 
@@ -689,7 +827,7 @@
     matrix = P("fsdp", None)
     weights = (vector, vector, matrix, vector, vector, matrix, vector, vector, vector, matrix, vector, matrix, vector)
     return jax.shard_map(
-        shards,
+        functools.partial(shards, mesh.shape["dp"]),
         mesh=mesh,
         in_specs=(rows, rows, P(None, ("dp", "fsdp"), None)) + weights,
         out_specs=(rows, rows) + weights,

time: 361 us -> 197 us (0.55)
  waiting for transfers between devices: 223 us -> 61.2 us
  starting transfers between devices: 0.31 us -> 43.8 us
  blocking collectives: 39.5 us -> 0 us
  local copies, waits for them, and re-layouts: 10.6 us -> 29.6 us
  between operations: 14.3 us -> 1.2 us
  Pallas kernels: 67.7 us -> 56.2 us
    reduce_scatter x4 -> x0, waiting for transfers between devices: 107 us -> none  [scatter(): own = lax.psum_scatter(value, 'fsdp', scatter_dimension=0, tiled=True)]
    all_gather x3 -> x0, waiting for transfers between devices: 75.1 us -> none  [gather(): whole = lax.all_gather(piece, 'fsdp', axis=0, tiled=True)]
    ppermute x0 -> x53, waiting for transfers between devices: none -> 61.2 us  [the longest x45 32.4 us: along(): return lax.ppermute(value, 'fsdp', [(i, i ^ offset) for i in range(8)])]
    ppermute x0 -> x53, starting transfers between devices: none -> 43.8 us  [the longest x45 33.1 us: along(): return lax.ppermute(value, 'fsdp', [(i, i ^ offset) for i in range(8)])]
    psum x1 -> x0, blocking collectives: 39.5 us -> none  [shards(): small = lax.psum(small, ('dp', 'fsdp'))]
    psum x1 -> x0, waiting for transfers between devices: 37.9 us -> none  [scatter(): return lax.psum(own, 'dp').astype(F32)]
    unnamed x15 -> x82, local copies, waits for them, and re-layouts: 5.99 us -> 24 us
    convert_element_type x3 -> x9, other arithmetic: 4.98 us -> 1.16 us  [the longest x3 0.77 us: scatter(): held = plus(here, along(there, 1)).astype(BF)]
  transfers between devices with their start and end apart: 8 -> 53, of which waited for: 7 -> 25; matrix products, arithmetic and copies ran while one was open for 1% -> 4% of each run, Pallas kernels for 11% -> 8%
where the time goes in v2:
time: 197 us; the launch traced here: 196 us
  waiting for transfers between devices  61.2 us (31%)
  Pallas kernels  56.2 us (29%)
  starting transfers between devices  43.8 us (22%)
  local copies, waits for them, and re-layouts  29.6 us (15%)
  other arithmetic  4.01 us (2%)
    ppermute x45, starting transfers between devices, along(): return lax.ppermute(value, 'fsdp', [(i, i ^ offset) for i in range(8)])  33.1 us
    ppermute x45, waiting for transfers between devices, along(): return lax.ppermute(value, 'fsdp', [(i, i ^ offset) for i in range(8)])  32.4 us
    ppermute x8, waiting for transfers between devices, across(): return lax.ppermute(value, 'dp', [(i, i ^ offset) for i in range(size)])  28.8 us
    unnamed x82, local copies, waits for them, and re-layouts  24 us
    pallas_call x1, Pallas kernels, rear(): pl.pallas_call(body, grid=(rows,), in_specs=[by_row(length, model), by_ro...  15.7 us
    pallas_call x1, Pallas kernels, middle(): pl.pallas_call(body, in_specs=[VMEM] * 3 + [HBM] * (len(up_parts) + len(d...  12.6 us
    pallas_call x1, Pallas kernels, front(): pl.pallas_call(body, grid=(rows,), in_specs=[pl.BlockSpec(memory_space=pl...  12.5 us
    pallas_call x1, Pallas kernels, back(): pl.pallas_call(body, in_specs=[VMEM] * 6 + [HBM] * (len(up_parts) + len(o...  11.6 us
  transfers between devices with their start and end apart: 53, of which 25 were waited for; matrix products, arithmetic and copies ran while one was open for 4% of the time, Pallas kernels for 8%

profile of v2, /device:TPU:0, one launch (start us, length us, event | category | flops | bytes accessed | tf_op | source)
XLA Modules:
  0.0 196.0 jit_solution(17229241758279726266)
XLA Ops:
  1.2 2.6 %collective-permute-start.10 = (bf16[64,2048]{1,0:T(8,128)(2,1)}, bf16[64,2048]{1,0:T(8,128)(2,1)S(1)}, u32[]{:S(2)}, u32[]{:S(2)}) collective-permute-start(bf16[64,2048]{1,0:T(8,128)(2,1)} %refs_0_.7), channel_id=1, source_target_pairs={{0,2},{1,3},{2,0},{3,1},{4,6},{5,7},{6,4},{7,5},{8,10},{9,11},{10,... | collective-permute-start | bytes 786440 | tf_op jit(solution)/shard_map/ppermute | solution.py:660
  13.7 1.9 collective-permute-start.1
  19.8 3.5 %collective-permute-done.1.refs_2_.refs_12_ = bf16[272,512]{1,0:T(8,128)(2,1)S(1)} collective-permute-done((bf16[272,512]{1,0:T(8,128)(2,1)S(1)}, bf16[272,512]{1,0:T(8,128)(2,1)S(1)}, u32[]{:S(2)}, u32[]{:S(2)}) %collective-permute-start.1) | collective-permute-done | bytes 278560 | tf_op jit(solution)/shard_map/ppermute | solution.py:660
  23.3 1.9 collective-permute-start.23
  28.5 2.3 %collective-permute-done.23.refs_16_.refs_6_ = bf16[128,512]{1,0:T(8,128)(2,1)S(1)} collective-permute-done((bf16[128,512]{1,0:T(8,128)(2,1)S(1)}, bf16[128,512]{1,0:T(8,128)(2,1)S(1)}, u32[]{:S(2)}, u32[]{:S(2)}) %collective-permute-start.23) | collective-permute-done | bytes 131104 | tf_op jit(solution)/shard_map/ppermute | solution.py:660
  33.1 2.8 %collective-permute-done.6.refs_7_.refs_17_ = bf16[144,512]{1,0:T(8,128)(2,1)S(1)} collective-permute-done((bf16[144,512]{1,0:T(8,128)(2,1)S(1)}, bf16[144,512]{1,0:T(8,128)(2,1)S(1)}, u32[]{:S(2)}, u32[]{:S(2)}) %collective-permute-start.6) | collective-permute-done | bytes 147488 | tf_op jit(solution)/shard_map/ppermute | solution.py:660
  38.9 12.5 %front.1 = (f32[16,512]{1,0:T(8,128)S(1)}, bf16[2,384,512]{2,1,0:T(8,128)(2,1)S(1)}, bf16[2,432,512]{2,1,0:T(8,128)(2,1)S(1)}, bf16[2,432,512]{2,1,0:T(8,128)(2,...) custom-call(s32[2,24]{1,0:T(2,128)S(1)} %bitcast.100, ...), custom_call_target="tpu_custom_call" | custom-call | flops 16099999744 | tf_op jit(solution)/shard_map/front/pallas_call | solution.py:224
  51.5 12.6 %middle.1 = (bf16[768,2048]{1,0:T(8,128)(2,1)S(1)}, bf16[768,2048]{1,0:T(8,128)(2,1)S(1)}, f32[4,512]{1,0:T(4,128)S(1)}, bf16[8,256,256]{2,1,0:T(8,128)(2,1)S(1)}, bf16[8,256,256]{2,1,0:T(8,128)(2,1)S(1)}) custom-call(bf16[768,512]{1,0:T(8,128)(2,1)S(1)} %bitcast.104, bf16[768,512]{1,0:T(8,128)(2,1)S(1)} %bitcast.96, f32[16,512]{1,0:T(8,128)S(1)} %get-tuple-element.38.vecs, ...), custom_call_target="tpu_custom_call" | custom-call | flops 18400000000 | tf_op jit(solution)/shard_map/middle/pallas_call | solution.py:347
  66.9 11.6 %back.1 = (f32[768,512]{1,0:T(8,128)S(1)}, bf16[768,512]{1,0:T(8,128)(2,1)S(1)}, f32[4,512]{1,0:T(4,128)S(1)}, bf16[8,32,2560]{2,1,0:T(8,128)(2,1)S(1)}, bf16[8,32,2560]{2,1,0:T(8,128)(2,1)S(1)}) custom-call(bf16[768,512]{1,0:T(8,128)(2,1)S(1)} %bitcast.105, bf16[768,2048]{1,0:T(8,128)(2,1)S(1)} %get-tuple-element.45.du, f32[768,512]{1,0:T(8,128)S(1)} %bitcast.101, ...), custom_call_target="tpu_custom_call" | custom-call | flops 14949999616 | tf_op jit(solution)/shard_map/back/pallas_call | solution.py:449
  79.5 15.7 %rear.1 = (f32[2,384,512]{2,1,0:T(8,128)}, f32[4,512]{1,0:T(4,128)S(1)}, bf16[8,32,1536]{2,1,0:T(8,128)(2,1)S(1)}, bf16[8,32,1536]{2,1,0:T(8,128)(2,1)S(1)}) custom-call(bf16[2,384,512]{2,1,0:T(8,128)(2,1)S(1)} %get-tuple-element.41.q, bf16[2,432,512]{2,1,0:T(8,128)(2,1)S(1)} %get-tuple-element.42.k, bf16[2,432,512]{2,1,0:T(8,128)(2,1)S(1)} %get-tuple-element.43.v, ...), custom_call_target="tpu_custom_call" | custom-call | flops 19549999104 | tf_op jit(solution)/shard_map/rear/pallas_call | solution.py:597
  98.4 3.1 %collective-permute-done.28 = f32[12,512]{1,0:T(8,128)S(1)} collective-permute-done((f32[12,512]{1,0:T(8,128)S(1)}, f32[12,512]{1,0:T(8,128)S(1)}, u32[]{:S(2)}, u32[]{:S(2)}) %collective-permute-start.28) | collective-permute-done | bytes 24608 | tf_op jit(solution)/shard_map/ppermute | solution.py:660
  103.0 2.4 %collective-permute-done.29 = f32[12,512]{1,0:T(8,128)S(1)} collective-permute-done((f32[12,512]{1,0:T(8,128)S(1)}, f32[12,512]{1,0:T(8,128)S(1)}, u32[]{:S(2)}, u32[]{:S(2)}) %collective-permute-start.29) | collective-permute-done | bytes 24608 | tf_op jit(solution)/shard_map/ppermute | solution.py:660
  108.1 2.1 %collective-permute-done.30 = f32[12,512]{1,0:T(8,128)} collective-permute-done((f32[12,512]{1,0:T(8,128)}, f32[12,512]{1,0:T(8,128)}, u32[]{:S(2)}, u32[]{:S(2)}) %collective-permute-start.30) | collective-permute-done | bytes 24608 | tf_op jit(solution)/shard_map/ppermute | solution.py:664
  111.0 2.6 %collective-permute-start.31 = (f32[12,512]{1,0:T(8,128)S(1)}, f32[12,512]{1,0:T(8,128)S(1)}, u32[]{:S(2)}, u32[]{:S(2)}) collective-permute-start(f32[12,512]{1,0:T(8,128)S(1)} %add.136), channel_id=1, source_target_pairs={{0,16},{8,24},{16,0},{24,8},{1,17},{9,25},{17,1},{25,9},{2,18},{10... | collective-permute-start | bytes 73736 | tf_op jit(solution)/shard_map/ppermute | solution.py:664
  122.5 1.9 copy-done.37
  125.1 3.7 %finish.1 = bf16[768,512]{1,0:T(8,128)(2,1)} custom-call(bf16[768,2048]{1,0:T(8,128)(2,1)S(1)} %copy-done.37, f32[768,512]{1,0:T(8,128)S(1)} %bitcast.102, f32[16,512]{1,0:T(8,128)S(1)} %copy-done.39, bf16[256,512]{1,0:T(8,128)(2,1)S(1)} %copy-done.9, bf16[256,512]{1,0:T(8,128)(2,1)S(1)} %copy-done.11, ...), custom_call_target="tpu_custom_call" | custom-call | flops 6899999744 | tf_op jit(solution)/shard_map/finish/pallas_call | solution.py:647
  134.6 2.2 %collective-permute-done.33 = bf16[2,32,1536]{2,1,0:T(8,128)(2,1)S(1)} collective-permute-done((bf16[2,32,1536]{2,1,0:T(8,128)(2,1)S(1)}, bf16[2,32,1536]{2,1,0:T(8,128)(2,1)S(1)}, u32[]{:S(2)}, u32[]{:S(2)}) %collective-permute-start.33) | collective-permute-done | bytes 196640 | tf_op jit(solution)/shard_map/ppermute | solution.py:660
  147.3 2.8 %collective-permute-start.37 = (bf16[2,32,1536]{2,1,0:T(8,128)(2,1)S(1)}, bf16[2,32,1536]{2,1,0:T(8,128)(2,1)S(1)}, u32[]{:S(2)}, u32[]{:S(2)}) collective-permute-start(bf16[2,32,1536]{2,1,0:T(8,128)(2,1)S(1)} %pad_maximum_fusion.2), channel_id=1, source_target_pairs={{0,8},{8,0},{16,24},{24,16},{1,9},{9,1},{17,25},{25,17},{2,10},{10... | collective-permute-start | bytes 589832 | tf_op jit(solution)/shard_map/ppermute | solution.py:664
  153.0 3.7 %collective-permute-done.40 = bf16[2,32,2560]{2,1,0:T(8,128)(2,1)S(1)} collective-permute-done((bf16[2,32,2560]{2,1,0:T(8,128)(2,1)S(1)}, bf16[2,32,2560]{2,1,0:T(8,128)(2,1)S(1)}, u32[]{:S(2)}, u32[]{:S(2)}) %collective-permute-start.40) | collective-permute-done | bytes 327712 | tf_op jit(solution)/shard_map/ppermute | solution.py:660
  160.3 2.0 %collective-permute-done.41 = bf16[32,2560]{1,0:T(8,128)(2,1)S(1)} collective-permute-done((bf16[32,2560]{1,0:T(8,128)(2,1)S(1)}, bf16[32,2560]{1,0:T(8,128)(2,1)S(1)}, u32[]{:S(2)}, u32[]{:S(2)}) %collective-permute-start.41) | collective-permute-done | bytes 163872 | tf_op jit(solution)/shard_map/ppermute | solution.py:660
  165.3 5.6 %collective-permute-done.51 = bf16[2,256,256]{2,1,0:T(8,128)(2,1)S(1)} collective-permute-done((bf16[2,256,256]{2,1,0:T(8,128)(2,1)S(1)}, bf16[2,256,256]{2,1,0:T(8,128)(2,1)S(1)}, u32[]{:S(2)}, u32[]{:S(2)}) %collective-permute-start.51) | collective-permute-done | bytes 262176 | tf_op jit(solution)/shard_map/ppermute | solution.py:664
  171.1 5.6 %collective-permute-done.44 = bf16[2,32,2560]{2,1,0:T(8,128)(2,1)S(1)} collective-permute-done((bf16[2,32,2560]{2,1,0:T(8,128)(2,1)S(1)}, bf16[2,32,2560]{2,1,0:T(8,128)(2,1)S(1)}, u32[]{:S(2)}, u32[]{:S(2)}) %collective-permute-start.44) | collective-permute-done | bytes 327712 | tf_op jit(solution)/shard_map/ppermute | solution.py:664
  178.5 12.4 %collective-permute-done.52 = bf16[2,256,256]{2,1,0:T(8,128)(2,1)S(1)} collective-permute-done((bf16[2,256,256]{2,1,0:T(8,128)(2,1)S(1)}, bf16[2,256,256]{2,1,0:T(8,128)(2,1)S(1)}, u32[]{:S(2)}, u32[]{:S(2)}) %collective-permute-start.52) | collective-permute-done | bytes 262176 | tf_op jit(solution)/shard_map/ppermute | solution.py:664
  192.0 2.4 %collective-permute-done.45 = bf16[2,32,2560]{2,1,0:T(8,128)(2,1)S(1)} collective-permute-done((bf16[2,32,2560]{2,1,0:T(8,128)(2,1)S(1)}, bf16[2,32,2560]{2,1,0:T(8,128)(2,1)S(1)}, u32[]{:S(2)}, u32[]{:S(2)}) %collective-permute-start.45) | collective-permute-done | bytes 327712 | tf_op jit(solution)/shard_map/ppermute | solution.py:664
  (212 shorter events, 75.0 us)
Async XLA Ops:
  1.2 12.6 %collective-permute-start.10 = (bf16[64,2048]{1,0:T(8,128)(2,1)}, bf16[64,2048]{1,0:T(8,128)(2,1)S(1)}, u32[]{:S(2)}, u32[]{:S(2)}) collective-permute-start(bf16[64,2048]{1,0:T(8,128)(2,1)} %refs_0_.7), channel_id=1, source_target_pairs={{0,2},{1,3},{2,0},{3,1},{4,6},{5,7},{6,4},{7,5},{8,10},{9,11},{10,... | collective-permute-start | bytes 786440 | tf_op jit(solution)/shard_map/ppermute | solution.py:660
  3.7 11.9 %collective-permute-start.11 = (bf16[64,2048]{1,0:T(8,128)(2,1)}, bf16[64,2048]{1,0:T(8,128)(2,1)S(1)}, u32[]{:S(2)}, u32[]{:S(2)}) collective-permute-start(bf16[64,2048]{1,0:T(8,128)(2,1)} %refs_0_.7), channel_id=1, source_target_pairs={{0,4},{1,5},{2,6},{3,7},{4,0},{5,1},{6,2},{7,3},{8,12},{9,13},{10,... | collective-permute-start | bytes 786440 | tf_op jit(solution)/shard_map/ppermute | solution.py:660
  5.3 10.4 %collective-permute-start.18 = (bf16[256,512]{1,0:T(8,128)(2,1)}, bf16[256,512]{1,0:T(8,128)(2,1)S(1)}, u32[]{:S(2)}, u32[]{:S(2)}) collective-permute-start(bf16[256,512]{1,0:T(8,128)(2,1)} %refs_0_.6), channel_id=1, source_target_pairs={{0,1},{1,0},{2,3},{3,2},{4,5},{5,4},{6,7},{7,6},{8,9},{9,8},{10,11... | collective-permute-start | bytes 786440 | tf_op jit(solution)/shard_map/ppermute | solution.py:660
  5.3 12.0 %collective-permute-start.19 = (bf16[256,512]{1,0:T(8,128)(2,1)}, bf16[256,512]{1,0:T(8,128)(2,1)S(1)}, u32[]{:S(2)}, u32[]{:S(2)}) collective-permute-start(bf16[256,512]{1,0:T(8,128)(2,1)} %refs_0_.6), channel_id=1, source_target_pairs={{0,2},{1,3},{2,0},{3,1},{4,6},{5,7},{6,4},{7,5},{8,10},{9,11},{10,... | collective-permute-start | bytes 786440 | tf_op jit(solution)/shard_map/ppermute | solution.py:660
  5.8 12.5 %collective-permute-start.20 = (bf16[256,512]{1,0:T(8,128)(2,1)}, bf16[256,512]{1,0:T(8,128)(2,1)S(1)}, u32[]{:S(2)}, u32[]{:S(2)}) collective-permute-start(bf16[256,512]{1,0:T(8,128)(2,1)} %refs_0_.6), channel_id=1, source_target_pairs={{0,4},{1,5},{2,6},{3,7},{4,0},{5,1},{6,2},{7,3},{8,12},{9,13},{10,... | collective-permute-start | bytes 786440 | tf_op jit(solution)/shard_map/ppermute | solution.py:660
  15.6 11.1 %collective-permute-start.2 = (bf16[272,512]{1,0:T(8,128)(2,1)S(1)}, bf16[272,512]{1,0:T(8,128)(2,1)S(1)}, u32[]{:S(2)}, u32[]{:S(2)}) collective-permute-start(bf16[272,512]{1,0:T(8,128)(2,1)S(1)} %pack.1.refs_0_.refs_10_), channel_id=1, source_target_pairs={{0,4},{1,5},{2,6},{3,7},{4,0},{5,1},{6,2},{7,3},{8,12},{9,13},{10,... | collective-permute-start | bytes 835592 | tf_op jit(solution)/shard_map/ppermute | solution.py:660
  17.3 10.7 %collective-permute-start.14 = (bf16[32,2048]{1,0:T(8,128)(2,1)S(1)}, bf16[32,2048]{1,0:T(8,128)(2,1)S(1)}, u32[]{:S(2)}, u32[]{:S(2)}) collective-permute-start(bf16[32,2048]{1,0:T(8,128)(2,1)S(1)} %slice.190), channel_id=1, source_target_pairs={{0,4},{1,5},{2,6},{3,7},{4,0},{5,1},{6,2},{7,3},{8,12},{9,13},{10,... | collective-permute-start | bytes 393224 | tf_op jit(solution)/shard_map/ppermute | solution.py:660
  37.5 13.9 %collective-permute-start.21 = (bf16[256,512]{1,0:T(8,128)(2,1)S(1)}, bf16[256,512]{1,0:T(8,128)(2,1)S(1)}, u32[]{:S(2)}, u32[]{:S(2)}) collective-permute-start(bf16[256,512]{1,0:T(8,128)(2,1)S(1)} %collective-permute-done.19.refs_12_.refs_2_), channel_id=1, source_target_pairs={{0,1},{1,0},{2,3},{3,2},{4,5},{5,4},{6,7},{7,6},{8,9},{9,8},{10,11... | collective-permute-start | bytes 786440 | tf_op jit(solution)/shard_map/ppermute | solution.py:660
  37.8 13.6 %collective-permute-start.22 = (bf16[256,512]{1,0:T(8,128)(2,1)S(1)}, bf16[256,512]{1,0:T(8,128)(2,1)S(1)}, u32[]{:S(2)}, u32[]{:S(2)}) collective-permute-start(bf16[256,512]{1,0:T(8,128)(2,1)S(1)} %collective-permute-done.20.refs_13_.refs_3_), channel_id=1, source_target_pairs={{0,1},{1,0},{2,3},{3,2},{4,5},{5,4},{6,7},{7,6},{8,9},{9,8},{10,11... | collective-permute-start | bytes 786440 | tf_op jit(solution)/shard_map/ppermute | solution.py:660
  38.0 13.4 %collective-permute-start.17 = (bf16[32,2048]{1,0:T(8,128)(2,1)S(1)}, bf16[32,2048]{1,0:T(8,128)(2,1)S(1)}, u32[]{:S(2)}, u32[]{:S(2)}) collective-permute-start(bf16[32,2048]{1,0:T(8,128)(2,1)S(1)} %collective-permute-done.15.refs_7_), channel_id=1, source_target_pairs={{0,1},{1,0},{2,3},{3,2},{4,5},{5,4},{6,7},{7,6},{8,9},{9,8},{10,11... | collective-permute-start | bytes 393224 | tf_op jit(solution)/shard_map/ppermute | solution.py:660
  38.3 13.1 %collective-permute-start.25 = (bf16[128,512]{1,0:T(8,128)(2,1)S(1)}, bf16[128,512]{1,0:T(8,128)(2,1)S(1)}, u32[]{:S(2)}, u32[]{:S(2)}) collective-permute-start(bf16[128,512]{1,0:T(8,128)(2,1)S(1)} %collective-permute-done.23.refs_16_.refs_6_), channel_id=1, source_target_pairs={{0,1},{1,0},{2,3},{3,2},{4,5},{5,4},{6,7},{7,6},{8,9},{9,8},{10,11... | collective-permute-start | bytes 393224 | tf_op jit(solution)/shard_map/ppermute | solution.py:660
  38.5 12.9 %collective-permute-start.26 = (bf16[128,512]{1,0:T(8,128)(2,1)S(1)}, bf16[128,512]{1,0:T(8,128)(2,1)S(1)}, u32[]{:S(2)}, u32[]{:S(2)}) collective-permute-start(bf16[128,512]{1,0:T(8,128)(2,1)S(1)} %collective-permute-done.24.refs_17_.refs_7_), channel_id=1, source_target_pairs={{0,1},{1,0},{2,3},{3,2},{4,5},{5,4},{6,7},{7,6},{8,9},{9,8},{10,11... | collective-permute-start | bytes 393224 | tf_op jit(solution)/shard_map/ppermute | solution.py:660
  107.6 23.2 %collective-permute-start.32 = (bf16[8,32,1536]{2,1,0:T(8,128)(2,1)}, bf16[8,32,1536]{2,1,0:T(8,128)(2,1)S(1)}, u32[]{:S(2)}, u32[]{:S(2)}) collective-permute-start(bf16[8,32,1536]{2,1,0:T(8,128)(2,1)} %copy-done.6), channel_id=1, source_target_pairs={{0,1},{1,0},{2,3},{3,2},{4,5},{5,4},{6,7},{7,6},{8,9},{9,8},{10,11... | collective-permute-start | bytes 2359304 | tf_op jit(solution)/shard_map/ppermute | solution.py:660
  107.6 38.0 %collective-permute-start.39 = (bf16[8,32,2560]{2,1,0:T(8,128)(2,1)}, bf16[8,32,2560]{2,1,0:T(8,128)(2,1)S(1)}, u32[]{:S(2)}, u32[]{:S(2)}) collective-permute-start(bf16[8,32,2560]{2,1,0:T(8,128)(2,1)} %copy-done.2), channel_id=1, source_target_pairs={{0,1},{1,0},{2,3},{3,2},{4,5},{5,4},{6,7},{7,6},{8,9},{9,8},{10,11... | collective-permute-start | bytes 3932168 | tf_op jit(solution)/shard_map/ppermute | solution.py:660
  108.1 32.6 %collective-permute-start.46 = (bf16[8,256,256]{2,1,0:T(8,128)(2,1)}, bf16[8,256,256]{2,1,0:T(8,128)(2,1)S(1)}, u32[]{:S(2)}, u32[]{:S(2)}) collective-permute-start(bf16[8,256,256]{2,1,0:T(8,128)(2,1)} %copy-done.3), channel_id=1, source_target_pairs={{0,1},{1,0},{2,3},{3,2},{4,5},{5,4},{6,7},{7,6},{8,9},{9,8},{10,11... | collective-permute-start | bytes 3145736 | tf_op jit(solution)/shard_map/ppermute | solution.py:660
  111.0 17.9 %collective-permute-start.31 = (f32[12,512]{1,0:T(8,128)S(1)}, f32[12,512]{1,0:T(8,128)S(1)}, u32[]{:S(2)}, u32[]{:S(2)}) collective-permute-start(f32[12,512]{1,0:T(8,128)S(1)} %add.136), channel_id=1, source_target_pairs={{0,16},{8,24},{16,0},{24,8},{1,17},{9,25},{17,1},{25,9},{2,18},{10... | collective-permute-start | bytes 73736 | tf_op jit(solution)/shard_map/ppermute | solution.py:664
  141.0 10.1 %collective-permute-start.47 = (bf16[2,256,256]{2,1,0:T(8,128)(2,1)S(1)}, bf16[2,256,256]{2,1,0:T(8,128)(2,1)S(1)}, u32[]{:S(2)}, u32[]{:S(2)}) collective-permute-start(bf16[2,256,256]{2,1,0:T(8,128)(2,1)S(1)} %get-tuple-element.84), channel_id=1, source_target_pairs={{0,2},{1,3},{2,0},{3,1},{4,6},{5,7},{6,4},{7,5},{8,10},{9,11},{10,... | collective-permute-start | bytes 786440 | tf_op jit(solution)/shard_map/ppermute | solution.py:660
  146.0 10.7 %collective-permute-start.40 = (bf16[2,32,2560]{2,1,0:T(8,128)(2,1)S(1)}, bf16[2,32,2560]{2,1,0:T(8,128)(2,1)S(1)}, u32[]{:S(2)}, u32[]{:S(2)}) collective-permute-start(bf16[2,32,2560]{2,1,0:T(8,128)(2,1)S(1)} %get-tuple-element.78), channel_id=1, source_target_pairs={{0,2},{1,3},{2,0},{3,1},{4,6},{5,7},{6,4},{7,5},{8,10},{9,11},{10,... | collective-permute-start | bytes 983048 | tf_op jit(solution)/shard_map/ppermute | solution.py:660
  147.3 17.5 %collective-permute-start.37 = (bf16[2,32,1536]{2,1,0:T(8,128)(2,1)S(1)}, bf16[2,32,1536]{2,1,0:T(8,128)(2,1)S(1)}, u32[]{:S(2)}, u32[]{:S(2)}) collective-permute-start(bf16[2,32,1536]{2,1,0:T(8,128)(2,1)S(1)} %pad_maximum_fusion.2), channel_id=1, source_target_pairs={{0,8},{8,0},{16,24},{24,16},{1,9},{9,1},{17,25},{25,17},{2,10},{10... | collective-permute-start | bytes 589832 | tf_op jit(solution)/shard_map/ppermute | solution.py:664
  159.2 11.7 %collective-permute-start.51 = (bf16[2,256,256]{2,1,0:T(8,128)(2,1)S(1)}, bf16[2,256,256]{2,1,0:T(8,128)(2,1)S(1)}, u32[]{:S(2)}, u32[]{:S(2)}) collective-permute-start(bf16[2,256,256]{2,1,0:T(8,128)(2,1)S(1)} %pad_maximum_fusion.1), channel_id=1, source_target_pairs={{0,8},{8,0},{16,24},{24,16},{1,9},{9,1},{17,25},{25,17},{2,10},{10... | collective-permute-start | bytes 786440 | tf_op jit(solution)/shard_map/ppermute | solution.py:664
  163.0 13.6 %collective-permute-start.44 = (bf16[2,32,2560]{2,1,0:T(8,128)(2,1)S(1)}, bf16[2,32,2560]{2,1,0:T(8,128)(2,1)S(1)}, u32[]{:S(2)}, u32[]{:S(2)}) collective-permute-start(bf16[2,32,2560]{2,1,0:T(8,128)(2,1)S(1)} %pad_maximum_fusion), channel_id=1, source_target_pairs={{0,8},{8,0},{16,24},{24,16},{1,9},{9,1},{17,25},{25,17},{2,10},{10... | collective-permute-start | bytes 983048 | tf_op jit(solution)/shard_map/ppermute | solution.py:664
  164.9 12.7 %collective-permute-start.38 = (bf16[2,32,1536]{2,1,0:T(8,128)(2,1)S(1)}, bf16[2,32,1536]{2,1,0:T(8,128)(2,1)S(1)}, u32[]{:S(2)}, u32[]{:S(2)}) collective-permute-start(bf16[2,32,1536]{2,1,0:T(8,128)(2,1)S(1)} %add_convert_fusion.5), channel_id=1, source_target_pairs={{0,16},{8,24},{16,0},{24,8},{1,17},{9,25},{17,1},{25,9},{2,18},{10... | collective-permute-start | bytes 589832 | tf_op jit(solution)/shard_map/ppermute | solution.py:664
  171.0 19.9 %collective-permute-start.52 = (bf16[2,256,256]{2,1,0:T(8,128)(2,1)S(1)}, bf16[2,256,256]{2,1,0:T(8,128)(2,1)S(1)}, u32[]{:S(2)}, u32[]{:S(2)}) collective-permute-start(bf16[2,256,256]{2,1,0:T(8,128)(2,1)S(1)} %add_convert_fusion.4), channel_id=1, source_target_pairs={{0,16},{8,24},{16,0},{24,8},{1,17},{9,25},{17,1},{25,9},{2,18},{10... | collective-permute-start | bytes 786440 | tf_op jit(solution)/shard_map/ppermute | solution.py:664
  176.7 17.7 %collective-permute-start.45 = (bf16[2,32,2560]{2,1,0:T(8,128)(2,1)S(1)}, bf16[2,32,2560]{2,1,0:T(8,128)(2,1)S(1)}, u32[]{:S(2)}, u32[]{:S(2)}) collective-permute-start(bf16[2,32,2560]{2,1,0:T(8,128)(2,1)S(1)} %add_convert_fusion.3), channel_id=1, source_target_pairs={{0,16},{8,24},{16,0},{24,8},{1,17},{9,25},{17,1},{25,9},{2,18},{10... | collective-permute-start | bytes 983048 | tf_op jit(solution)/shard_map/ppermute | solution.py:664
  (69 other events, 469.7 us)
